TPU v7x, 512 devices: a whole 4x8x8 slice. The times are simulated.
512 devices in a mesh: row: 32 (over y, x), col: 16 (over z, core).
Axes of the slice: x: 4, y: 8, z: 8, core: 2. Of those that a mesh axis runs over, the one named last changes fastest.
Arguments:
- source_features: bfloat16 [16, 2048, 256], P('col', 'row'), may hold values from -500 to 500
- target_features: bfloat16 [32768, 256], P(('row', 'col')), may hold values from -6 to 6
- weight: bfloat16 [256, 256], replicated, may hold values from -0.375 to 0.375
- score_source: float32 [4, 64], replicated, may hold values from -0.75 to 0.75
- score_target: float32 [4, 64], replicated, may hold values from -0.75 to 0.75
- out_bias: float32 [256], replicated, may hold values from -3 to 3
- block_list: int32 [32, 16, 48], P('row', 'col'), may hold values from 0 to 127, as said below
- block_count: int32 [32, 16], P('row', 'col'), may hold values from 8 to 48, as said below
- edge_bits: int32 [32, 16, 48, 16, 128], P('row', 'col'), may hold values from 0 to 255, as said below
Outputs:
- updated: bfloat16 [32768, 256], P(('row', 'col'))
Inputs may be any that keep to these rules, and one draw needn't show every extreme that they name: `block_list`: slot s of tile (r, c) names target block p // 16 and source block p % 16 of the tile; the first block_count[r, c] slots of a tile name distinct blocks and later slots are unused. `block_count`: some tile holds 48 blocks. `edge_bits`: bit b of entry [r, c, s, w, i] marks the edge from source 8 w + b to target i of the block in slot s. Some targets have no edge.
All inputs are finite; a program needn't handle non-finite values.
Results may differ from a plain program's by a relative error of at most 0.007.
The roundings to bfloat16 on the way count: a program that leaves them out, or rounds other values in their place, can miss the bound.
Values may be sent and summed in bfloat16 or wider, within the bound.
A program may use at most 64 MiB of HBM per device.

v0:
```python
import jax
import jax.numpy as jnp
from jax import lax
from jax.sharding import PartitionSpec as P

BLK = 128
SB = 16


very_low = -1e30
slope = 0.2


def unpack_all(packed):
    shifts = jnp.arange(8, dtype=jnp.int32)
    spread = jnp.right_shift(packed[:, :, None, :], shifts[None, None, :, None]) & 1
    return spread.reshape(packed.shape[0], packed.shape[1] * 8, packed.shape[2]) > 0


def all_scores(src_pick, dst_pick):
    raw = src_pick[:, :, :, None] + dst_pick[:, :, None, :]
    return jnp.where(raw > 0, raw, slope * raw)


def body(
    source_features,
    target_features,
    weight,
    score_source,
    score_target,
    out_bias,
    block_list,
    block_count,
    edge_bits,
):
    head_count = score_source.shape[0]
    head_size = score_source.shape[1]
    out_width = weight.shape[1]
    own_proj = jnp.dot(source_features[0], weight, preferred_element_type=jnp.float32).astype(
        jnp.bfloat16
    )
    projected = lax.all_gather(own_proj, "row", axis=0, tiled=True)
    src_logits = jnp.einsum(
        "nhk,hk->hn",
        projected.reshape(-1, head_count, head_size).astype(jnp.float32),
        score_source,
        precision=lax.Precision.HIGHEST,
    )
    dst_proj = jnp.dot(target_features, weight, preferred_element_type=jnp.float32)
    dst_local = jnp.einsum(
        "nhk,hk->hn",
        dst_proj.reshape(-1, head_count, head_size),
        score_target,
        precision=lax.Precision.HIGHEST,
    )
    dst_logits = lax.all_gather(dst_local, "col", axis=1, tiled=True)
    dst_rows = dst_logits.shape[1]
    dst_blocks_all = dst_rows // BLK
    src_blocks_all = src_logits.shape[1] // BLK
    slots = block_list[0, 0]
    live = block_count[0, 0]
    packed = edge_bits[0, 0]
    slot_count = slots.shape[0]
    dst_block = slots // SB
    src_block = slots % SB
    in_use = jnp.arange(slot_count, dtype=jnp.int32) < live
    edge_mask = unpack_all(packed) & in_use[:, None, None]
    src_pick = jnp.take(src_logits.reshape(head_count, src_blocks_all, BLK), src_block, axis=1)
    dst_pick = jnp.take(dst_logits.reshape(head_count, dst_blocks_all, BLK), dst_block, axis=1)
    owner = dst_block[:, None] == jnp.arange(dst_blocks_all, dtype=jnp.int32)[None, :]
    owner_float = owner.astype(jnp.float32)
    scores = all_scores(src_pick, dst_pick)
    block_max = jnp.max(jnp.where(edge_mask[None], scores, very_low), axis=2)
    spread_max = jnp.where(owner[None, :, :, None], block_max[:, :, None, :], very_low)
    row_max = jnp.max(spread_max, axis=1).reshape(head_count, dst_rows)
    row_max = lax.pmax(row_max, "col")
    prior_max = jnp.take(row_max.reshape(head_count, dst_blocks_all, BLK), dst_block, axis=1)
    scores = all_scores(src_pick, dst_pick)
    numer = jnp.exp(jnp.where(edge_mask[None], scores - prior_max[:, :, None, :], very_low))
    slot_denoms = jnp.sum(numer, axis=2)
    denoms = jnp.einsum(
        "sd,hsi->dih", owner_float, slot_denoms, precision=lax.Precision.HIGHEST
    ).reshape(dst_rows, head_count)
    weights = numer.astype(jnp.bfloat16)
    src_feats = jnp.take(
        projected.reshape(src_blocks_all, BLK, head_count, head_size), src_block, axis=0
    )
    product = jnp.einsum("hsji,sjhk->sihk", weights, src_feats, preferred_element_type=jnp.float32)
    accum = jnp.einsum(
        "sd,sihk->dihk", owner_float, product, precision=lax.Precision.HIGHEST
    ).reshape(dst_rows, out_width)
    accum, denoms = (
        lax.psum(accum.astype(jnp.bfloat16), "col").astype(jnp.float32),
        lax.psum(denoms.astype(jnp.bfloat16), "col").astype(jnp.float32),
    )
    own_count = dst_rows // lax.axis_size("col")
    first_row = lax.axis_index("col") * own_count
    accum = lax.dynamic_slice_in_dim(accum, first_row, own_count, 0)
    denoms = lax.dynamic_slice_in_dim(denoms, first_row, own_count, 0)
    own_count = accum.shape[0]
    blended = accum.reshape(own_count, head_count, head_size) / jnp.maximum(denoms, 1.0)[:, :, None]
    return jax.nn.elu(blended.reshape(own_count, out_width) + out_bias).astype(jnp.bfloat16)


def solution(mesh):
    placed = (
        P("col", "row", None),
        P(("row", "col"), None),
        P(),
        P(),
        P(),
        P(),
        P("row", "col", None),
        P("row", "col"),
        P("row", "col", None, None, None),
    )
    return jax.shard_map(
        body, mesh=mesh, in_specs=placed, out_specs=P(("row", "col"), None), check_vma=False
    )
```

profile of v0, /device:TPU:1, one launch (start us, length us, event | category | flops | bytes accessed | tf_op | source)
XLA Modules:
  0.0 296.6 jit_solution(9279656370350139183)
XLA Ops:
  6.5 0.9 copy-done
  7.4 1.5 convolution_convert_fusion
  9.0 0.9 fusion.45
  9.9 0.1 reshape.177
  10.1 1.0 fusion.28
  11.1 24.6 %all-gather = f32[16,64,4]{1,2,0:T(4,128)S(1)} all-gather(f32[1,64,4]{1,2,0:T(4,128)S(1)} %bitcast.101), channel_id=1, replica_groups=mesh['row'=32,'col'=16] {'col'}, dimensions={0}, use_global_device_ids=true | all-gather | bytes 17408 | tf_op jit(solution)/shard_map/all_gather | solution.py:56
  36.5 0.7 compare_and_fusion
  37.3 0.6 gather_fusion.2
  37.9 0.7 fusion.39
  38.6 1.9 fusion.17
  40.6 52.5 %all-gather.3.cloned.1.call-done = bf16[2048,256]{1,0:T(8,128)(2,1)} async-done(((bf16[64,256]{1,0:T(8,128)(2,1)}), bf16[2048,256]{1,0:T(8,128)(2,1)}) %all-gather.3.cloned.1.call-update) | async-done | bytes 1048592 | tf_op jit(solution)/shard_map/all_gather | solution.py:42
  93.1 1.6 copy.40
  94.7 1.2 fusion.44
  95.9 0.6 gather_fusion.1
  96.5 0.2 select_bitcast_fusion.1
  96.7 4.4 %select_reduce_fusion = f32[4,48,128]{2,0,1:T(4,128)S(1)} fusion(f32[4,48,128]{2,0,1:T(4,128)S(1)} %get-tuple-element.9, f32[4,48,128]{2,0,1:T(4,128)S(1)} %get-tuple-element.10, pred[48,128,128]{2,1,0:T(8,128)(4,1)S(1)} %fusion.17), kind=kLoop, calls=%fused_computation.6 | loop fusion | flops 18849792 | bytes 1081344 | tf_op jit(solution)/shard_map/reduce_max | solution.py:73
  101.1 0.1 select_reduce_fusion.1
  101.2 48.2 %pmax.7 = f32[4,8,128]{2,0,1:T(4,128)S(1)} all-reduce(f32[4,8,128]{2,0,1:T(4,128)S(1)} %copy.44), channel_id=1, replica_groups=mesh['row'=32,'col'=16] {'col'}, use_global_device_ids=true, to_apply=%region_2.4 | all-reduce | flops 4096 | bytes 32768 | tf_op jit(solution)/shard_map/pmax | solution.py:76
  149.4 0.6 gather_fusion.3
  150.1 0.8 select_bitcast_fusion
  150.8 0.8 reshape.228
  151.7 1.1 copy.39
  152.8 2.7 gather_fusion
  155.5 9.9 %fusion.18 = f32[48,128,4,64]{1,3,2,0:T(8,128)S(1)} fusion(f32[4,48,128]{2,0,1:T(4,128)S(1)} %copy-done.4, f32[4,48,128]{2,0,1:T(4,128)S(1)} %get-tuple-element.9, f32[4,48,128]{2,0,1:T(4,128)S(1)} %get-tuple-element.10, pred[48,128,128]{2,1,0:T(8,128)(4,1)S(1)} %copy-done.3, bf16[48,128,4,64]{1,3,2,0:T(8,128)(2,1)} %gather_fusion, ...), kind=kOutput, calls=%fused_computation.25 | convolution fusion | flops 426246144 | bytes 10518576 | tf_op jit(solution)/shard_map/hsji,sjhk->sihk/dot_general | solution.py:88
  165.4 5.7 %fusion.24 = bf16[8,128,4,64]{1,0,3,2:T(8,128)(2,1)S(1)} fusion(f32[48,128,4,64]{1,3,2,0:T(8,128)S(1)} %fusion.18, s32[48]{0:T(128)S(1)} %get-tuple-element.7), kind=kOutput, calls=%fused_computation.27 | convolution fusion | flops 151257472 | bytes 6815936 | tf_op jit(solution)/shard_map/sd,sihk->dihk/dot_general | solution.py:89
  171.2 1.0 copy.46
  172.2 5.5 %fusion = f32[4,48,128]{2,0,1:T(4,128)S(1)} fusion(f32[4,48,128]{2,0,1:T(4,128)S(1)} %copy-done.4, f32[4,48,128]{2,0,1:T(4,128)S(1)} %get-tuple-element.9, f32[4,48,128]{2,0,1:T(4,128)S(1)} %get-tuple-element.10, pred[48,128,128]{2,1,0:T(8,128)(4,1)S(1)} %copy-done.3), kind=kLoop, calls=%fused_computation.7 | loop fusion | flops 21995520 | bytes 1179648 | tf_op jit(solution)/shard_map/reduce_sum | solution.py:80
  177.7 0.2 fusion.27
  177.9 27.0 %psum.15 = bf16[1024,4]{0,1:T(4,128)(2,1)S(1)} all-reduce(bf16[1024,4]{0,1:T(4,128)(2,1)S(1)} %bitcast.100), channel_id=1, replica_groups=mesh['row'=32,'col'=16] {'col'}, use_global_device_ids=true, to_apply=%region_5.7 | all-reduce | flops 4096 | bytes 16384 | tf_op jit(solution)/shard_map/psum | solution.py:94
  205.2 0.1 div.28
  205.4 83.0 %all-reduce.2.cloned.1.call-done = bf16[1024,256]{1,0:T(8,128)(2,1)} async-done(((bf16[1024,256]{1,0:T(8,128)(2,1)}), bf16[1024,256]{1,0:T(8,128)(2,1)}) %all-reduce.2.cloned.1.call-update) | async-done | bytes 524304 | tf_op jit(solution)/shard_map/psum | solution.py:93
  288.3 1.4 fusion.32
  (33 shorter events, 0.8 us)
Async XLA Ops:
  6.5 0.9 copy-start
  6.5 86.5 %all-gather.3.cloned.1.call-start = ((), (), s32[]{:S(2)}) async-start(), calls=%async_computation | async-start | bytes 1081344 | tf_op jit(solution)/shard_map/all_gather | solution.py:42
  9.0 279.3 %all-reduce.2.cloned.1.call-start = ((), (), s32[]{:S(2)}) async-start(), calls=%async_computation.1 | async-start | bytes 1048576 | tf_op jit(solution)/shard_map/psum | solution.py:93
  40.6 109.5 %copy-start.2 = (pred[48,128,128]{2,1,0:T(8,128)(4,1)}, pred[48,128,128]{2,1,0:T(8,128)(4,1)S(1)}, u32[]{:S(2)}) copy-start(pred[48,128,128]{2,1,0:T(8,128)(4,1)S(1)} %fusion.17) | copy-start | bytes 2359300
  93.1 57.8 %copy-start.1 = (bf16[2048,256]{1,0:T(8,128)(2,1)S(1)}, bf16[2048,256]{1,0:T(8,128)(2,1)}, u32[]{:S(2)}) copy-start(bf16[2048,256]{1,0:T(8,128)(2,1)} %all-gather.3.cloned.1.call-done) | copy-start | bytes 3145732
  152.8 2.7 copy-start.3
  152.8 2.7 copy-start.4
  165.4 122.9 %copy-start.5 = (f32[256]{0:T(256)S(1)}, f32[256]{0:T(256)}, u32[]{:S(2)}) copy-start(f32[256]{0:T(256)} %param.16) | copy-start | bytes 3076
Sparse Core Ops, SparseCore 0:
  10.5 82.5 all-gather.2
  172.3 115.9 all-reduce.1
where the time goes:
time: 297 us
  waiting for transfers between devices  136 us (46%)
  blocking collectives  99.8 us (34%)
  matrix products  20.3 us (7%)
  other arithmetic  15.7 us (5%)
  between operations  14.3 us (5%)
  local copies, waits for them, and re-layouts  10.9 us (4%)
    psum x1, waiting for transfers between devices, body(): lax.psum(accum.astype(jnp.bfloat16), 'col').astype(jnp.float32)  83 us
    all_gather x1, waiting for transfers between devices, body(): projected = lax.all_gather(own_proj, 'row', axis=0, tiled=True)  52.5 us
    pmax x1, blocking collectives, body(): row_max = lax.pmax(row_max, 'col')  48.2 us
    psum x1, blocking collectives, body(): lax.psum(denoms.astype(jnp.bfloat16), 'col').astype(jnp.float32)  27 us
    all_gather x1, blocking collectives, body(): dst_logits = lax.all_gather(dst_local, 'col', axis=1, tiled=True)  24.6 us
    dot_general x1, matrix products, body(): jnp.einsum('hsji,sjhk->sihk', weights, src_feats, preferred_element_type=...  9.89 us
  transfers between devices with their start and end apart: 2, of which 2 were waited for; matrix products, arithmetic and copies ran while one was open for 4% of the time, Pallas kernels for 0%

commit v1 on v0

v1 whole, which is shorter than its diff:
```python
import functools

import jax
import jax.numpy as jnp
from jax import lax
from jax.experimental import pallas as pl
from jax.experimental.pallas import tpu as pltpu
from jax.sharding import PartitionSpec as P

BLK = 128
SB = 16
DB = 8
HEADS = 4
HD = 64
WIDTH = 256
ROWS = 32
COLS = 16
OWN = 64

very_low = -1e30
no_edge = -3e38
slope = 0.2
MESH = pl.DeviceIdType.MESH
by_columns = (((1,), (1,)), ((), ()))


def in_three(x):
    high = x.astype(jnp.bfloat16)
    rest = x - high.astype(jnp.float32)
    middle = rest.astype(jnp.bfloat16)
    low = (rest - middle.astype(jnp.float32)).astype(jnp.bfloat16)
    return high, middle, low


def leaky(x):
    return jnp.maximum(x, slope * x)


def gather_kernel(
    src_ref, tgt_ref, weight_ref, target_ref, feats_ref, logits_ref,
    own_ref, own_logits, send_a, recv_a, send_b, recv_b,
):
    row, col = lax.axis_index("row"), lax.axis_index("col")
    barrier = pltpu.get_barrier_semaphore()

    def greet_row(d, _):
        pl.semaphore_signal(barrier, inc=1, device_id=(lax.rem(row + d, ROWS), col), device_id_type=MESH)
        return 0

    def greet_col(d, _):
        pl.semaphore_signal(barrier, inc=1, device_id=(row, lax.rem(col + d, COLS)), device_id_type=MESH)
        return 0

    lax.fori_loop(1, ROWS, greet_row, 0)
    lax.fori_loop(1, COLS, greet_col, 0)
    own = jnp.dot(src_ref[...], weight_ref[...], preferred_element_type=jnp.float32)
    own_ref[...] = own.astype(jnp.bfloat16)
    product = jnp.dot(tgt_ref[...], weight_ref[...], preferred_element_type=jnp.float32) * target_ref[...]
    head_of = lax.broadcasted_iota(jnp.int32, (8, WIDTH), 1) // HD
    pick = (head_of == lax.broadcasted_iota(jnp.int32, (8, WIDTH), 0)).astype(jnp.bfloat16)
    high, middle, low = in_three(product)
    logits = lax.dot_general(pick, low, by_columns, preferred_element_type=jnp.float32)
    logits += lax.dot_general(pick, middle, by_columns, preferred_element_type=jnp.float32)
    logits += lax.dot_general(pick, high, by_columns, preferred_element_type=jnp.float32)
    twice = jnp.concatenate([logits, logits], axis=1)
    half = lax.broadcasted_iota(jnp.int32, (8, BLK), 1) // OWN
    own_logits[...] = jnp.where(half == lax.rem(col, 2), twice, 0.0)
    feats_ref[row] = own_ref[...]
    logits_ref[col] = own_logits[...]
    pl.semaphore_wait(barrier, ROWS + COLS - 2)

    def logits_copy(d):
        return pltpu.make_async_remote_copy(
            src_ref=own_logits, dst_ref=logits_ref.at[col], send_sem=send_b.at[d], recv_sem=recv_b.at[d],
            device_id=(row, lax.rem(col + d, COLS)), device_id_type=MESH,
        )

    def feats_copy(d):
        return pltpu.make_async_remote_copy(
            src_ref=own_ref, dst_ref=feats_ref.at[row], send_sem=send_a.at[d], recv_sem=recv_a.at[d],
            device_id=(lax.rem(row + d, ROWS), col), device_id_type=MESH,
        )

    def start_logits(d, _):
        logits_copy(d).start()
        return 0

    def start_feats(d, _):
        feats_copy(d).start()
        return 0

    def wait_logits(d, _):
        logits_copy(d).wait()
        return 0

    def wait_feats(d, _):
        feats_copy(d).wait()
        return 0

    lax.fori_loop(1, COLS, start_logits, 0)
    lax.fori_loop(1, ROWS, start_feats, 0)
    lax.fori_loop(1, COLS, wait_logits, 0)
    lax.fori_loop(1, ROWS, wait_feats, 0)


def gather(source, target, weight, score_target):
    vmem = pl.BlockSpec(memory_space=pltpu.VMEM)
    return pl.pallas_call(
        gather_kernel,
        out_shape=(
            jax.ShapeDtypeStruct((ROWS, OWN, WIDTH), jnp.bfloat16),
            jax.ShapeDtypeStruct((COLS, 8, BLK), jnp.float32),
        ),
        in_specs=[vmem] * 4,
        out_specs=(vmem, vmem),
        scratch_shapes=[
            pltpu.VMEM((OWN, WIDTH), jnp.bfloat16),
            pltpu.VMEM((8, BLK), jnp.float32),
            pltpu.SemaphoreType.DMA((ROWS,)),
            pltpu.SemaphoreType.DMA((ROWS,)),
            pltpu.SemaphoreType.DMA((COLS,)),
            pltpu.SemaphoreType.DMA((COLS,)),
        ],
        compiler_params=pltpu.CompilerParams(collective_id=0, has_side_effects=True, vmem_limit_bytes=16 << 20),
        name="gather",
    )(source, target, weight, score_target)


def tile_kernel(
    slots_ref, live_ref, feats_ref, logits_ref, bits_ref, source_ref, sums_ref, maxima_ref,
    turned, spread, dst, best, total, accum, weights,
):
    live = live_ref[0]
    head_of = lax.broadcasted_iota(jnp.int32, (BLK, WIDTH), 1) // HD
    pick = head_of == lax.broadcasted_iota(jnp.int32, (BLK, WIDTH), 0)
    score = in_three(jnp.where(pick, source_ref[...], 0.0))
    eye = (lax.broadcasted_iota(jnp.int32, (WIDTH, WIDTH), 0) == lax.broadcasted_iota(jnp.int32, (WIDTH, WIDTH), 1)).astype(jnp.bfloat16)
    for d in range(DB):
        dst[d] = logits_ref[2 * d] + logits_ref[2 * d + 1]
    best[...] = jnp.full(best.shape, no_edge, jnp.float32)
    total[...] = jnp.zeros(total.shape, jnp.float32)
    accum[...] = jnp.zeros(accum.shape, jnp.float32)

    @pl.loop(0, SB)
    def _(s):
        rows = pl.ds(pl.multiple_of(s * BLK, BLK), BLK)
        block = feats_ref[rows, :]
        flipped = lax.dot_general(eye, block, by_columns, preferred_element_type=jnp.float32)
        turned[s] = flipped.astype(jnp.bfloat16)
        logits = lax.dot_general(block, score[2], by_columns, preferred_element_type=jnp.float32)
        logits += lax.dot_general(block, score[1], by_columns, preferred_element_type=jnp.float32)
        logits += lax.dot_general(block, score[0], by_columns, preferred_element_type=jnp.float32)
        for h in range(HEADS):
            spread[h, rows, :] = jnp.broadcast_to(logits[:, h : h + 1], (BLK, BLK))

    bit = jnp.left_shift(1, lax.broadcasted_iota(jnp.int32, (8, BLK), 0))

    def edges(slot, w):
        words = bits_ref[slot, pl.ds(w, 1), :]
        return (jnp.broadcast_to(words, (8, BLK)) & bit) != 0

    @pl.loop(0, live)
    def _(slot):
        place = slots_ref[slot]
        d, s = place // SB, lax.rem(place, SB)
        top = [best[d, h] for h in range(HEADS)]
        for w in range(BLK // 8):
            mask = edges(slot, w)
            rows = pl.ds(pl.multiple_of(s * BLK + 8 * w, 8), 8)
            for h in range(HEADS):
                top[h] = jnp.maximum(top[h], jnp.where(mask, spread[h, rows, :], no_edge))
        for h in range(HEADS):
            best[d, h] = top[h]

    maxima_ref[...] = jnp.zeros(maxima_ref.shape, jnp.float32)
    for d in range(DB):
        for h in range(HEADS):
            top = jnp.max(best[d, h], axis=0, keepdims=True)
            value = leaky(top + dst[d, h : h + 1, :])
            maxima_ref[d, h : h + 1, :] = jnp.where(top > -1e38, value, very_low)

    @pl.loop(0, live)
    def _(slot):
        place = slots_ref[slot]
        d, s = place // SB, lax.rem(place, SB)
        sums = [total[d, h] for h in range(HEADS)]
        b = [jnp.broadcast_to(dst[d, pl.ds(h, 1), :], (8, BLK)) for h in range(HEADS)]
        m = [jnp.broadcast_to(maxima_ref[d, pl.ds(h, 1), :], (8, BLK)) for h in range(HEADS)]
        for w in range(0, BLK // 8, 2):
            masks = [edges(slot, w), edges(slot, w + 1)]
            for h in range(HEADS):
                pair = []
                for half in range(2):
                    rows = pl.ds(pl.multiple_of(s * BLK + 8 * (w + half), 8), 8)
                    score = leaky(spread[h, rows, :] + b[h]) - m[h]
                    numer = jnp.where(masks[half], jnp.exp(score), 0.0)
                    sums[h] = sums[h] + numer
                    pair.append(numer)
                weights[h, 8 * w : 8 * w + 16, :] = jnp.concatenate(pair, axis=0).astype(jnp.bfloat16)
        for h in range(HEADS):
            total[d, h] = sums[h]
            part = jnp.dot(turned[s, h * HD : (h + 1) * HD, :], weights[h], preferred_element_type=jnp.float32)
            accum[d, h * HD : (h + 1) * HD, :] += part

    for d in range(DB):
        for h in range(HEADS):
            maxima_ref[d, HEADS + h : HEADS + h + 1, :] = jnp.sum(total[d, h], axis=0, keepdims=True)
        back = lax.dot_general(
            eye[:BLK, :BLK], accum[d].astype(jnp.bfloat16), by_columns, preferred_element_type=jnp.float32
        ).astype(jnp.bfloat16)
        sums_ref[2 * d] = back[:OWN]
        sums_ref[2 * d + 1] = back[OWN:]


def attend(slots, live, feats, logits, bits, score_source):
    vmem = pl.BlockSpec(memory_space=pltpu.VMEM)
    smem = pl.BlockSpec(memory_space=pltpu.SMEM)
    return pl.pallas_call(
        tile_kernel,
        out_shape=(
            jax.ShapeDtypeStruct((COLS, OWN, WIDTH), jnp.bfloat16),
            jax.ShapeDtypeStruct((DB, 8, BLK), jnp.float32),
        ),
        in_specs=[smem, smem, vmem, vmem, vmem, vmem],
        out_specs=(vmem, vmem),
        scratch_shapes=[
            pltpu.VMEM((SB, WIDTH, BLK), jnp.bfloat16),
            pltpu.VMEM((HEADS, SB * BLK, BLK), jnp.float32),
            pltpu.VMEM((DB, 8, BLK), jnp.float32),
            pltpu.VMEM((DB, HEADS, 8, BLK), jnp.float32),
            pltpu.VMEM((DB, HEADS, 8, BLK), jnp.float32),
            pltpu.VMEM((DB, WIDTH, BLK), jnp.float32),
            pltpu.VMEM((HEADS, BLK, BLK), jnp.bfloat16),
        ],
        compiler_params=pltpu.CompilerParams(vmem_limit_bytes=32 << 20),
        name="attend",
    )(slots, live, feats, logits, bits, score_source)


def combine_kernel(
    sums_ref, maxima_ref, bias_ref, out_ref, got_sums, got_max, send_a, recv_a, send_b, recv_b,
):
    row, col = lax.axis_index("row"), lax.axis_index("col")
    barrier = pltpu.get_barrier_semaphore()

    def greet(d, _):
        pl.semaphore_signal(barrier, inc=1, device_id=(row, lax.rem(col + d, COLS)), device_id_type=MESH)
        return 0

    lax.fori_loop(1, COLS, greet, 0)
    got_sums[col] = sums_ref[col]
    got_max[col] = maxima_ref[col // 2]
    pl.semaphore_wait(barrier, COLS - 1)

    def max_copy(d):
        peer = lax.rem(col + d, COLS)
        return pltpu.make_async_remote_copy(
            src_ref=maxima_ref.at[peer // 2], dst_ref=got_max.at[col], send_sem=send_b.at[d], recv_sem=recv_b.at[d],
            device_id=(row, peer), device_id_type=MESH,
        )

    def sums_copy(d):
        peer = lax.rem(col + d, COLS)
        return pltpu.make_async_remote_copy(
            src_ref=sums_ref.at[peer], dst_ref=got_sums.at[col], send_sem=send_a.at[d], recv_sem=recv_a.at[d],
            device_id=(row, peer), device_id_type=MESH,
        )

    def start_max(d, _):
        max_copy(d).start()
        return 0

    def start_sums(d, _):
        sums_copy(d).start()
        return 0

    def wait_max(d, _):
        max_copy(d).wait()
        return 0

    def wait_sums(d, _):
        sums_copy(d).wait()
        return 0

    lax.fori_loop(1, COLS, start_max, 0)
    lax.fori_loop(1, COLS, start_sums, 0)
    lax.fori_loop(1, COLS, wait_max, 0)
    every = got_max[...]
    local = every[:, :HEADS, :]
    top = jnp.max(local, axis=0, keepdims=True)
    factor = jnp.exp(local - top)
    denoms = jnp.sum(factor * every[:, HEADS:, :], axis=0, keepdims=True)
    factor = factor / jnp.maximum(denoms, 1.0)
    flat = jnp.concatenate([factor[c] for c in range(COLS)] + [jnp.zeros((BLK - COLS * HEADS, BLK), jnp.float32)], axis=0)
    turned = flat.T
    turned = jnp.where(lax.rem(col, 2) == 0, turned[:OWN], turned[OWN:])
    lax.fori_loop(1, COLS, wait_sums, 0)
    parts = [jnp.zeros((OWN, HD), jnp.float32)] * HEADS
    for c in range(COLS):
        for h in range(HEADS):
            scale = jnp.broadcast_to(turned[:, c * HEADS + h : c * HEADS + h + 1], (OWN, HD))
            parts[h] = parts[h] + scale * got_sums[c, :, h * HD : (h + 1) * HD].astype(jnp.float32)
    blended = jnp.concatenate(parts, axis=1) + bias_ref[...]
    result = jnp.where(blended > 0, blended, jnp.exp(jnp.minimum(blended, 0.0)) - 1.0)
    out_ref[...] = result.astype(jnp.bfloat16)


def combine(sums, maxima, bias):
    vmem = pl.BlockSpec(memory_space=pltpu.VMEM)
    return pl.pallas_call(
        combine_kernel,
        out_shape=jax.ShapeDtypeStruct((OWN, WIDTH), jnp.bfloat16),
        in_specs=[vmem] * 3,
        out_specs=vmem,
        scratch_shapes=[
            pltpu.VMEM((COLS, OWN, WIDTH), jnp.bfloat16),
            pltpu.VMEM((COLS, 8, BLK), jnp.float32),
            pltpu.SemaphoreType.DMA((COLS,)),
            pltpu.SemaphoreType.DMA((COLS,)),
            pltpu.SemaphoreType.DMA((COLS,)),
            pltpu.SemaphoreType.DMA((COLS,)),
        ],
        compiler_params=pltpu.CompilerParams(collective_id=1, has_side_effects=True, vmem_limit_bytes=16 << 20),
        name="combine",
    )(sums, maxima, bias)


def body(
    source_features, target_features, weight, score_source, score_target, out_bias,
    block_list, block_count, edge_bits,
):
    feats, logits = gather(source_features[0], target_features, weight, score_target.reshape(1, WIDTH))
    sums, maxima = attend(
        block_list[0, 0], block_count[0], feats.reshape(SB * BLK, WIDTH), logits, edge_bits[0, 0],
        score_source.reshape(1, WIDTH),
    )
    return combine(sums, maxima, out_bias.reshape(1, WIDTH))


def solution(mesh):
    placed = (
        P("col", "row", None),
        P(("row", "col"), None),
        P(),
        P(),
        P(),
        P(),
        P("row", "col", None),
        P("row", "col"),
        P("row", "col", None, None, None),
    )
    return jax.shard_map(
        body, mesh=mesh, in_specs=placed, out_specs=P(("row", "col"), None), check_vma=False
    )
```

time: 297 us -> 88.6 us (0.30)
  the two profiles are of different devices: /device:TPU:1 before, /device:TPU:7 now
where the time goes in v1:
time: 88.6 us; the launch traced here: 88.2 us
  Pallas kernels  81.3 us (92%)
  local copies, waits for them, and re-layouts  6.19 us (7%)
    pallas_call x1, Pallas kernels, gather(): pl.pallas_call(gather_kernel, out_shape=(jax.ShapeDtypeStruct((ROWS, OWN,...  38.7 us
    pallas_call x1, Pallas kernels, combine(): pl.pallas_call(combine_kernel, out_shape=jax.ShapeDtypeStruct((OWN, WIDTH...  22.9 us
    pallas_call x1, Pallas kernels, attend(): pl.pallas_call(tile_kernel, out_shape=(jax.ShapeDtypeStruct((COLS, OWN, W...  19.6 us
    unnamed x17, local copies, waits for them, and re-layouts  6.03 us

profile of v1, /device:TPU:7, one launch (start us, length us, event | category | flops | bytes accessed | tf_op | source)
XLA Modules:
  0.0 88.2 jit_solution(8674590373155435371)
XLA Ops:
  0.7 0.0 copy-start.6
  0.7 0.0 copy-start.7
  0.7 0.7 copy-done.6
  1.3 0.1 reshape.14.source_ref
  1.4 0.0 copy-done.7
  1.4 0.1 reshape.12.target_ref
  1.5 0.0 copy-start.1
  1.5 0.9 %copy-done.1 = bf16[256,256]{1,0:T(8,128)(2,1)S(1)} copy-done((bf16[256,256]{1,0:T(8,128)(2,1)S(1)}, bf16[256,256]{1,0:T(8,128)(2,1)}, u32[]{:S(2)}) %copy-start.1) | copy-done | bytes 131096
  2.4 0.0 copy-start.2
  2.4 0.8 copy-done.2
  3.2 0.0 copy-start.3
  3.2 0.8 copy-done.3
  3.9 38.7 %gather.1 = (bf16[32,64,256]{2,1,0:T(8,128)(2,1)S(1)}, f32[16,8,128]{2,1,0:T(8,128)S(1)}) custom-call(bf16[64,256]{1,0:T(8,128)(2,1)S(1)} %bitcast.9, bf16[64,256]{1,0:T(8,128)(2,1)S(1)} %copy-done.3, bf16[256,256]{1,0:T(8,128)(2,1)S(1)} %copy-done.1, f32[1,256]{1,0:T(1,128)S(1)} %reshape.12.target_ref), custom_call_target="tpu_custom_call" | custom-call | tf_op jit(solution)/shard_map/gather/pallas_call | solution.py:108
  42.7 0.0 copy-start.5
  42.7 0.6 copy-done.5
  43.3 0.0 copy-start
  43.3 1.0 %copy-done = s32[1,1,48,16,128]{4,3,2,1,0:T(8,128)S(1)} copy-done((s32[1,1,48,16,128]{4,3,2,1,0:T(8,128)S(1)}, s32[1,1,48,16,128]{4,3,2,1,0:T(8,128)}, u32[]{:S(2)}) %copy-start) | copy-done | bytes 393240
  44.3 19.6 %attend.1 = (bf16[16,64,256]{2,1,0:T(8,128)(2,1)S(1)}, f32[8,8,128]{2,1,0:T(8,128)S(1)}) custom-call(s32[48]{0:T(128)S(1)} %bitcast.11, s32[1]{0:T(128)} %bitcast.6.live_ref, bf16[2048,256]{1,0:T(8,128)(2,1)S(1)} %bitcast.7, f32[16,8,128]{2,1,0:T(8,128)S(1)} %get-tuple-element.10.logits_ref, s32[48,16,128]{2,1,0:T(8,128)S(1)} %bitcast.8, ...), custom_call_target="tpu_custom_call" | custom-call | tf_op jit(solution)/shard_map/attend/pallas_call | solution.py:218
  64.0 0.0 copy-start.4
  64.0 0.7 copy-done.4
  64.7 22.9 %combine.1 = bf16[64,256]{1,0:T(8,128)(2,1)S(1)} custom-call(bf16[16,64,256]{2,1,0:T(8,128)(2,1)S(1)} %get-tuple-element.11.sums_ref, f32[8,8,128]{2,1,0:T(8,128)S(1)} %get-tuple-element.12.maxima_ref, f32[1,256]{1,0:T(1,128)S(1)} %bitcast.10), custom_call_target="tpu_custom_call" | custom-call | tf_op jit(solution)/shard_map/combine/pallas_call | solution.py:310
  87.6 0.6 copy.12
Async XLA Ops:
  0.7 0.7 copy-start.6
  0.7 0.8 copy-start.7
  1.5 0.9 %copy-start.1 = (bf16[256,256]{1,0:T(8,128)(2,1)S(1)}, bf16[256,256]{1,0:T(8,128)(2,1)}, u32[]{:S(2)}) copy-start(bf16[256,256]{1,0:T(8,128)(2,1)} %weight_ref.1) | copy-start | bytes 393220
  2.4 0.8 copy-start.2
  3.2 0.8 copy-start.3
  42.7 0.7 copy-start.5
  43.3 1.0 %copy-start = (s32[1,1,48,16,128]{4,3,2,1,0:T(8,128)S(1)}, s32[1,1,48,16,128]{4,3,2,1,0:T(8,128)}, u32[]{:S(2)}) copy-start(s32[1,1,48,16,128]{4,3,2,1,0:T(8,128)} %param.17) | copy-start | bytes 1179652
  64.0 0.7 copy-start.4

commit v2 on v0

v2 whole, which is shorter than its diff:
```python
import jax
import jax.numpy as jnp
from jax import lax
from jax.experimental import pallas as pl
from jax.experimental.pallas import tpu as pltpu
from jax.sharding import PartitionSpec as P

BLK = 128
SB = 16
DB = 8
SLOTS = 48
HEADS = 4
HD = 64
WIDTH = 256
ROWS = 32
COLS = 16
XS = 4
YS = 8
ZS = 8
OWN = 64

very_low = -1e30
no_edge = -3e38
slope = 0.2
MESH = pl.DeviceIdType.MESH
by_columns = (((1,), (1,)), ((), ()))


def in_three(x):
    high = x.astype(jnp.bfloat16)
    rest = x - high.astype(jnp.float32)
    middle = rest.astype(jnp.bfloat16)
    low = (rest - middle.astype(jnp.float32)).astype(jnp.bfloat16)
    return low, middle, high


def leaky(x):
    return jnp.maximum(x, slope * x)


def loop(first, last, step):
    def one(i, _):
        step(i)
        return 0

    lax.fori_loop(first, last, one, 0)


def in_half(rows, position):
    twice = jnp.concatenate([rows, rows], axis=1)
    half = lax.broadcasted_iota(jnp.int32, (8, BLK), 1) // OWN
    return jnp.where(half == lax.rem(position, 2), twice, 0.0)


def flat_scores(ref):
    return jnp.concatenate([ref[h : h + 1, :] for h in range(HEADS)], axis=1)


def scores_kernel(
    src_hbm, tgt_hbm, weight_hbm, source_hbm, target_hbm, slots_hbm, live_hbm, bits_hbm,
    u_ref, v_ref, weights_ref, sums_ref, maxima_ref,
    src_ref, tgt_ref, weight_ref, source_ref, target_ref, slots_ref, live_ref, bits_ref,
    src_rows, dst_rows, spread, dst, tops, best,
    local, send_a, recv_a, send_b, recv_b, send_x, recv_x, send_y, recv_y,
    send_up, recv_up, send_down, recv_down, send_f, recv_f,
):
    row, col = lax.axis_index("row"), lax.axis_index("col")
    x, y = lax.rem(row, XS), row // XS
    pairs = (
        (weight_hbm, weight_ref), (src_hbm, src_ref), (tgt_hbm, tgt_ref), (source_hbm, source_ref),
        (target_hbm, target_ref), (slots_hbm, slots_ref), (live_hbm, live_ref), (bits_hbm, bits_ref),
    )
    loads = [pltpu.make_async_copy(a, b, local.at[i]) for i, (a, b) in enumerate(pairs)]
    for load in loads:
        load.start()
    barrier = pltpu.get_barrier_semaphore()

    def greet_row(d):
        pl.semaphore_signal(barrier, inc=1, device_id=(lax.rem(row + d, ROWS), col), device_id_type=MESH)

    def greet_col(d):
        pl.semaphore_signal(barrier, inc=1, device_id=(row, lax.rem(col + d, COLS)), device_id_type=MESH)

    loop(1, ROWS, greet_row)
    loop(1, COLS, greet_col)

    for load in loads[:5]:
        load.wait()
    own = jnp.dot(src_ref[...], weight_ref[...], preferred_element_type=jnp.float32).astype(jnp.bfloat16)
    u_ref[row] = own[:, :BLK]
    v_ref[row] = own[:, BLK:]
    head_of = lax.broadcasted_iota(jnp.int32, (8, WIDTH), 1) // HD
    pick = head_of == lax.broadcasted_iota(jnp.int32, (8, WIDTH), 0)
    parts = in_three(jnp.where(pick, flat_scores(source_ref), 0.0))
    logits = [lax.dot_general(part, own, by_columns, preferred_element_type=jnp.float32) for part in parts]
    src_rows[row] = in_half(logits[0] + logits[1] + logits[2], row)
    product = jnp.dot(tgt_ref[...], weight_ref[...], preferred_element_type=jnp.float32) * flat_scores(target_ref)
    ones = pick.astype(jnp.bfloat16)
    logits = [lax.dot_general(ones, part, by_columns, preferred_element_type=jnp.float32) for part in in_three(product)]
    dst_rows[col] = in_half(logits[0] + logits[1] + logits[2], col)
    pl.semaphore_wait(barrier, ROWS + COLS - 2)

    def source_logits(d):
        return pltpu.make_async_remote_copy(
            src_ref=src_rows.at[row], dst_ref=src_rows.at[row], send_sem=send_a.at[d], recv_sem=recv_a.at[d],
            device_id=(lax.rem(row + d, ROWS), col), device_id_type=MESH,
        )

    def target_logits(d):
        return pltpu.make_async_remote_copy(
            src_ref=dst_rows.at[col], dst_ref=dst_rows.at[col], send_sem=send_b.at[d], recv_sem=recv_b.at[d],
            device_id=(row, lax.rem(col + d, COLS)), device_id_type=MESH,
        )

    def along_x(d):
        return pltpu.make_async_remote_copy(
            src_ref=u_ref.at[row], dst_ref=u_ref.at[row], send_sem=send_x.at[d], recv_sem=recv_x.at[d],
            device_id=(y * XS + lax.rem(x + d, XS), col), device_id_type=MESH,
        )

    def along_y(d):
        return pltpu.make_async_remote_copy(
            src_ref=v_ref.at[row], dst_ref=v_ref.at[row], send_sem=send_y.at[d], recv_sem=recv_y.at[d],
            device_id=(lax.rem(y + d, YS) * XS + x, col), device_id_type=MESH,
        )

    def up(k):
        first = lax.rem(y - (k - 1) + YS, YS) * XS
        part = pl.ds(first, XS if k < YS // 2 else XS // 2)
        return pltpu.make_async_remote_copy(
            src_ref=u_ref.at[part], dst_ref=u_ref.at[part], send_sem=send_up.at[k], recv_sem=recv_up.at[k],
            device_id=(lax.rem(y + 1, YS) * XS + x, col), device_id_type=MESH,
        )

    def down(k):
        first = lax.rem(y + (k - 1), YS) * XS
        part = pl.ds(first, XS) if k < YS // 2 else pl.ds(first + XS // 2, XS // 2)
        return pltpu.make_async_remote_copy(
            src_ref=u_ref.at[part], dst_ref=u_ref.at[part], send_sem=send_down.at[k], recv_sem=recv_down.at[k],
            device_id=(lax.rem(y + YS - 1, YS) * XS + x, col), device_id_type=MESH,
        )

    def onward(d, e):
        block = lax.rem(y - d + YS, YS) * XS + x
        return pltpu.make_async_remote_copy(
            src_ref=v_ref.at[block], dst_ref=v_ref.at[block], send_sem=send_f.at[d, e], recv_sem=recv_f.at[d, e],
            device_id=(y * XS + lax.rem(x + e, XS), col), device_id_type=MESH,
        )

    def hand_on(d):
        along_y(d).wait_recv()
        for e in range(1, XS):
            onward(d, e).start()

    def ring(k):
        if k > 1:
            up(k - 1).wait_recv()
            down(k - 1).wait_recv()
        up(k).start()
        down(k).start()

    loop(1, ROWS, lambda d: source_logits(d).start())
    for d in range(1, XS):
        along_x(d).start()
        onward(0, d).start()
    for d in (1, 7, 2, 6, 3, 5, 4):
        along_y(d).start()
    loop(1, COLS, lambda d: target_logits(d).start())

    for load in loads[5:]:
        load.wait()
    live = live_ref[0, 0]
    for d in range(1, XS):
        along_x(d).wait_recv()
    ring(1)
    loop(1, ROWS, lambda d: source_logits(d).wait_recv())
    everyone = jnp.concatenate([src_rows[2 * s] + src_rows[2 * s + 1] for s in range(SB)], axis=0).T
    for s in range(SB):
        for h in range(HEADS):
            spread[h, s] = jnp.broadcast_to(everyone[:, 8 * s + h : 8 * s + h + 1], (BLK, BLK))
    hand_on(1)
    hand_on(7)
    ring(2)

    bit = jnp.left_shift(1, lax.broadcasted_iota(jnp.int32, (8, BLK), 0))

    def edges(slot, w, bit):
        words = bits_ref[slot, pl.ds(w, 1), :]
        return (jnp.broadcast_to(words, (8, BLK)) & bit) != 0

    def slot_max(slot):
        s = slots_ref[0, slot] & (SB - 1)
        used = bit & (jnp.clip(live - slot, 0, 1) * 255)
        top = [jnp.full((8, BLK), no_edge, jnp.float32)] * HEADS
        for w in range(BLK // 8):
            mask = edges(slot, w, used)
            for h in range(HEADS):
                top[h] = jnp.maximum(top[h], jnp.where(mask, spread[h, s, 8 * w : 8 * w + 8, :], no_edge))
        for h in range(HEADS):
            tops[slot, h] = top[h]

    loop(0, SLOTS // 2, slot_max)
    for d in (2, 6, 3, 5, 4):
        hand_on(d)
    ring(3)
    loop(SLOTS // 2, SLOTS, slot_max)

    for h in range(HEADS):
        def widen(slot, found):
            d_here = jnp.full((8, BLK), jnp.right_shift(slots_ref[0, slot], 4), jnp.int32)
            top = tops[slot, h]
            return tuple(
                jnp.maximum(old, jnp.where(d_here == d, top, no_edge)) for d, old in enumerate(found)
            )

        found = lax.fori_loop(0, SLOTS, widen, (jnp.full((8, BLK), no_edge, jnp.float32),) * DB)
        for d in range(DB):
            best[d, h] = found[d]
    loop(1, COLS, lambda d: target_logits(d).wait_recv())
    for d in range(DB):
        dst[d] = dst_rows[2 * d] + dst_rows[2 * d + 1]
        values = []
        for h in range(HEADS):
            top = jnp.max(best[d, h], axis=0, keepdims=True)
            values.append(jnp.where(top > -1e38, leaky(top + dst[d, h : h + 1, :]), very_low))
        maxima_ref[d] = jnp.concatenate(values * 2, axis=0)
    ring(4)

    def slot_weights(slot):
        place = slots_ref[0, slot]
        d, s = jnp.right_shift(place, 4), place & (SB - 1)
        used = bit & (jnp.clip(live - slot, 0, 1) * 255)
        sums = [jnp.zeros((8, BLK), jnp.float32)] * HEADS
        b = [jnp.broadcast_to(dst[d, h : h + 1, :], (8, BLK)) for h in range(HEADS)]
        m = [jnp.broadcast_to(maxima_ref[d, h : h + 1, :], (8, BLK)) for h in range(HEADS)]
        for w in range(0, BLK // 8, 2):
            masks = [edges(slot, w, used), edges(slot, w + 1, used)]
            for h in range(HEADS):
                pair = []
                for half in range(2):
                    from_src = spread[h, s, 8 * (w + half) : 8 * (w + half) + 8, :]
                    score = leaky(from_src + b[h]) - m[h]
                    numer = jnp.where(masks[half], jnp.exp(score), 0.0)
                    sums[h] = sums[h] + numer
                    pair.append(numer)
                weights_ref[slot, h, 8 * w : 8 * w + 16, :] = jnp.concatenate(pair, axis=0).astype(jnp.bfloat16)
        for h in range(HEADS):
            sums_ref[slot, h] = sums[h]

    loop(0, SLOTS, slot_weights)

    loop(1, ROWS, lambda d: source_logits(d).wait_send())
    loop(1, COLS, lambda d: target_logits(d).wait_send())
    for d in range(1, XS):
        along_x(d).wait_send()
    for k in range(1, YS // 2 + 1):
        up(k).wait_send()
        down(k).wait_send()
    up(YS // 2).wait_recv()
    down(YS // 2).wait_recv()
    for d in range(YS):
        if d:
            along_y(d).wait_send()
        for e in range(1, XS):
            onward(d, e).wait()


def scores(source, target, weight, score_source, score_target, slots, live, bits):
    vmem = pl.BlockSpec(memory_space=pltpu.VMEM)
    anywhere = pl.BlockSpec(memory_space=pl.ANY)
    dma = pltpu.SemaphoreType.DMA
    return pl.pallas_call(
        scores_kernel,
        out_shape=(
            jax.ShapeDtypeStruct((ROWS, OWN, BLK), jnp.bfloat16),
            jax.ShapeDtypeStruct((ROWS, OWN, BLK), jnp.bfloat16),
            jax.ShapeDtypeStruct((SLOTS, HEADS, BLK, BLK), jnp.bfloat16),
            jax.ShapeDtypeStruct((SLOTS, HEADS, 8, BLK), jnp.float32),
            jax.ShapeDtypeStruct((DB, 8, BLK), jnp.float32),
        ),
        in_specs=[anywhere] * 8,
        out_specs=(vmem,) * 5,
        scratch_shapes=[
            pltpu.VMEM((OWN, WIDTH), jnp.bfloat16),
            pltpu.VMEM((OWN, WIDTH), jnp.bfloat16),
            pltpu.VMEM((WIDTH, WIDTH), jnp.bfloat16),
            pltpu.VMEM((HEADS, HD), jnp.float32),
            pltpu.VMEM((HEADS, HD), jnp.float32),
            pltpu.SMEM((1, SLOTS), jnp.int32),
            pltpu.SMEM((1, 1), jnp.int32),
            pltpu.VMEM((SLOTS, BLK // 8, BLK), jnp.int32),
            pltpu.VMEM((ROWS, 8, BLK), jnp.float32),
            pltpu.VMEM((COLS, 8, BLK), jnp.float32),
            pltpu.VMEM((HEADS, SB, BLK, BLK), jnp.float32),
            pltpu.VMEM((DB, 8, BLK), jnp.float32),
            pltpu.VMEM((SLOTS, HEADS, 8, BLK), jnp.float32),
            pltpu.VMEM((DB, HEADS, 8, BLK), jnp.float32),
            dma((8,)),
            dma((ROWS,)), dma((ROWS,)),
            dma((COLS,)), dma((COLS,)),
            dma((XS,)), dma((XS,)),
            dma((YS,)), dma((YS,)),
            dma((YS,)), dma((YS,)),
            dma((YS,)), dma((YS,)),
            dma((YS, XS)), dma((YS, XS)),
        ],
        compiler_params=pltpu.CompilerParams(collective_id=0, has_side_effects=True, vmem_limit_bytes=32 << 20),
        name="scores",
    )(source, target, weight, score_source, score_target, slots, live, bits)


def sums_kernel(slots_ref, u_ref, v_ref, weights_ref, parts_ref, maxima_ref, accum_ref, stats_ref, turned, accum, total):
    eye = (
        lax.broadcasted_iota(jnp.int32, (BLK, BLK), 0) == lax.broadcasted_iota(jnp.int32, (BLK, BLK), 1)
    ).astype(jnp.bfloat16)
    for s in range(SB):
        for i, ref in enumerate((u_ref, v_ref)):
            block = ref[s * BLK : (s + 1) * BLK, :]
            flipped = lax.dot_general(eye, block, by_columns, preferred_element_type=jnp.float32)
            turned[s, i * BLK : (i + 1) * BLK, :] = flipped.astype(jnp.bfloat16)
    total[...] = jnp.zeros(total.shape, jnp.float32)
    accum[...] = jnp.zeros(accum.shape, jnp.float32)

    @pl.loop(0, SLOTS, unroll=UNROLL)
    def _(slot):
        place = slots_ref[0, slot]
        d, s = place // SB, lax.rem(place, SB)
        for h in range(HEADS):
            part = jnp.dot(turned[s, h * HD : (h + 1) * HD, :], weights_ref[slot, h], preferred_element_type=jnp.float32)
            accum[d, h * HD : (h + 1) * HD, :] += part
            total[d, h] += parts_ref[slot, h]

    for d in range(DB):
        accum_ref[d] = accum[d].astype(jnp.bfloat16)
        rows = [maxima_ref[d, :HEADS, :]] + [jnp.sum(total[d, h], axis=0, keepdims=True) for h in range(HEADS)]
        stats_ref[d] = jnp.concatenate(rows, axis=0)


UNROLL = 4


def sums(slots, u, v, weights, parts, maxima):
    vmem = pl.BlockSpec(memory_space=pltpu.VMEM)
    smem = pl.BlockSpec(memory_space=pltpu.SMEM)
    return pl.pallas_call(
        sums_kernel,
        out_shape=(
            jax.ShapeDtypeStruct((DB, WIDTH, BLK), jnp.bfloat16),
            jax.ShapeDtypeStruct((DB, 8, BLK), jnp.float32),
        ),
        in_specs=[smem] + [vmem] * 5,
        out_specs=(vmem, vmem),
        scratch_shapes=[
            pltpu.VMEM((SB, WIDTH, BLK), jnp.bfloat16),
            pltpu.VMEM((DB, WIDTH, BLK), jnp.float32),
            pltpu.VMEM((DB, HEADS, 8, BLK), jnp.float32),
        ],
        compiler_params=pltpu.CompilerParams(vmem_limit_bytes=24 << 20),
        name="sums",
    )(slots, u, v, weights, parts, maxima)


def combine_kernel(
    accum_ref, stats_ref, bias_ref, out_ref, twin_accum, twin_stats, got, got_stats, half_ref, twin_half,
    send_p, recv_p, send_q, recv_q, send_a, recv_a, send_b, recv_b, send_o, recv_o, joint, joint_stats,
):
    row, col = lax.axis_index("row"), lax.axis_index("col")
    z, core = col // 2, lax.rem(col, 2)
    twin = (row, col + 1 - 2 * core)
    barrier = pltpu.get_barrier_semaphore()
    pl.semaphore_signal(barrier, inc=1, device_id=twin, device_id_type=MESH)

    def peer(d):
        return (row, lax.rem(z + d, ZS) * 2 + core)

    loop(1, ZS, lambda d: pl.semaphore_signal(barrier, inc=1, device_id=peer(d), device_id_type=MESH))
    pl.semaphore_wait(barrier, ZS)

    theirs = pl.ds(pl.multiple_of((1 - core) * BLK, BLK), BLK)
    mine = pl.ds(pl.multiple_of(core * BLK, BLK), BLK)

    def stats_copy():
        return pltpu.make_async_remote_copy(
            src_ref=stats_ref, dst_ref=twin_stats, send_sem=send_q, recv_sem=recv_q, device_id=twin, device_id_type=MESH,
        )

    def pair_copy(d):
        return pltpu.make_async_remote_copy(
            src_ref=accum_ref.at[d, theirs], dst_ref=twin_accum.at[d], send_sem=send_p.at[d], recv_sem=recv_p.at[d],
            device_id=twin, device_id_type=MESH,
        )

    def joint_copy(d):
        there = lax.rem(z + d, ZS)
        return pltpu.make_async_remote_copy(
            src_ref=joint.at[there], dst_ref=got.at[z], send_sem=send_a.at[d], recv_sem=recv_a.at[d],
            device_id=peer(d), device_id_type=MESH,
        )

    def joint_stats_copy(d):
        there = lax.rem(z + d, ZS)
        return pltpu.make_async_remote_copy(
            src_ref=joint_stats.at[there], dst_ref=got_stats.at[z], send_sem=send_b.at[d], recv_sem=recv_b.at[d],
            device_id=peer(d), device_id_type=MESH,
        )

    order = (4, 3, 5, 2, 6, 1, 7, 0)
    stats_copy().start()
    for d in order:
        pair_copy(lax.rem(z + d, ZS)).start()
    stats_copy().wait_recv()

    def own_heads(tile):
        return jnp.where(core == 0, tile[0:2], tile[2:4]), jnp.where(core == 0, tile[4:6], tile[6:8])

    for d in order:
        there = lax.rem(z + d, ZS)
        m0, s0 = own_heads(stats_ref[there])
        m1, s1 = own_heads(twin_stats[there])
        m = jnp.maximum(m0, m1)
        f0, f1 = jnp.exp(m0 - m), jnp.exp(m1 - m)
        tile = jnp.concatenate([m, s0 * f0 + s1 * f1, m, m], axis=0)
        pair_copy(there).wait_recv()
        mixed = []
        for h in range(2):
            rows = pl.ds(pl.multiple_of(core * BLK + h * HD, HD), HD)
            mine_part = accum_ref[there, rows, :].astype(jnp.float32)
            twin_part = twin_accum[there, h * HD : (h + 1) * HD, :].astype(jnp.float32)
            mixed.append(mine_part * f0[h : h + 1] + twin_part * f1[h : h + 1])
        mixed = jnp.concatenate(mixed, axis=0).astype(jnp.bfloat16)
        if d:
            joint_stats[there] = tile
            joint[there] = mixed
            joint_stats_copy(d).start()
            joint_copy(d).start()
        else:
            got_stats[z] = tile
            got[z] = mixed

    for d in range(1, ZS):
        joint_stats_copy(d).wait_recv()
    every = got_stats[...]
    local = every[:, 0:2, :]
    top = jnp.max(local, axis=0, keepdims=True)
    factor = jnp.exp(local - top)
    denoms = jnp.sum(factor * every[:, 2:4, :], axis=0, keepdims=True)
    factor = factor / jnp.maximum(denoms, 1.0)
    for d in range(1, ZS):
        joint_copy(d).wait_recv()
    parts = []
    for h in range(2):
        part = jnp.zeros((HD, BLK), jnp.float32)
        for c in range(ZS):
            part = part + factor[c, h : h + 1, :] * got[c, h * HD : (h + 1) * HD, :].astype(jnp.float32)
        parts.append(part)
    turned = jnp.concatenate(parts, axis=0).T
    bias = jnp.where(core == 0, bias_ref[:, :BLK], bias_ref[:, BLK:])
    blended = turned + bias
    result = jnp.where(blended > 0, blended, jnp.exp(jnp.minimum(blended, 0.0)) - 1.0).astype(jnp.bfloat16)
    half_ref[...] = jnp.where(core == 0, result[OWN:], result[:OWN])
    swap = pltpu.make_async_remote_copy(
        src_ref=half_ref, dst_ref=twin_half, send_sem=send_o, recv_sem=recv_o, device_id=twin, device_id_type=MESH,
    )
    swap.start()
    out_ref[:, mine] = jnp.where(core == 0, result[:OWN], result[OWN:])
    for d in range(1, ZS):
        joint_stats_copy(d).wait_send()
        joint_copy(d).wait_send()
    stats_copy().wait_send()
    loop(0, ZS, lambda d: pair_copy(d).wait_send())
    swap.wait()
    out_ref[:, theirs] = twin_half[...]


def combine(accum, stats, bias):
    vmem = pl.BlockSpec(memory_space=pltpu.VMEM)
    dma = pltpu.SemaphoreType.DMA
    return pl.pallas_call(
        combine_kernel,
        out_shape=jax.ShapeDtypeStruct((OWN, WIDTH), jnp.bfloat16),
        in_specs=[vmem] * 3,
        out_specs=vmem,
        scratch_shapes=[
            pltpu.VMEM((ZS, BLK, BLK), jnp.bfloat16),
            pltpu.VMEM((ZS, 8, BLK), jnp.float32),
            pltpu.VMEM((ZS, BLK, BLK), jnp.bfloat16),
            pltpu.VMEM((ZS, 8, BLK), jnp.float32),
            pltpu.VMEM((OWN, BLK), jnp.bfloat16),
            pltpu.VMEM((OWN, BLK), jnp.bfloat16),
            dma((ZS,)), dma((ZS,)),
            dma, dma,
            dma((ZS,)), dma((ZS,)),
            dma((ZS,)), dma((ZS,)),
            dma, dma,
            pltpu.VMEM((ZS, BLK, BLK), jnp.bfloat16),
            pltpu.VMEM((ZS, 8, BLK), jnp.float32),
        ],
        compiler_params=pltpu.CompilerParams(collective_id=1, has_side_effects=True, vmem_limit_bytes=16 << 20),
        name="combine",
    )(accum, stats, bias)


def body(
    source_features, target_features, weight, score_source, score_target, out_bias,
    block_list, block_count, edge_bits,
):
    slots = block_list[0]
    u, v, weights, parts, maxima = scores(
        source_features[0], target_features, weight, score_source, score_target, slots, block_count, edge_bits[0, 0]
    )
    flat = (SB * BLK, BLK)
    accum, stats = sums(slots, u.reshape(flat), v.reshape(flat), weights, parts, maxima)
    return combine(accum, stats, out_bias.reshape(1, WIDTH))


def solution(mesh):
    placed = (
        P("col", "row", None),
        P(("row", "col"), None),
        P(),
        P(),
        P(),
        P(),
        P("row", "col", None),
        P("row", "col"),
        P("row", "col", None, None, None),
    )
    return jax.shard_map(
        body, mesh=mesh, in_specs=placed, out_specs=P(("row", "col"), None), check_vma=False
    )
```

time: 297 us -> 68.8 us (0.23)
  waiting for transfers between devices: 136 us -> 0 us
  blocking collectives: 99.8 us -> 0 us
  Pallas kernels: 0 us -> 61 us
  matrix products: 20.3 us -> 0 us
  other arithmetic: 15.7 us -> 0 us
  between operations: 14.3 us -> 0.72 us
  local copies, waits for them, and re-layouts: 10.9 us -> 6.7 us
    psum x1 -> x0, waiting for transfers between devices: 83 us -> none  [body(): lax.psum(accum.astype(jnp.bfloat16), 'col').astype(jnp.float32)]
    pallas_call x0 -> x3, Pallas kernels: none -> 61 us  [the longest x1 37 us: scores(): pl.pallas_call(scores_kernel, out_shape=(jax.ShapeDtypeStruct((ROWS, OWN,...]
    all_gather x1 -> x0, waiting for transfers between devices: 52.5 us -> none  [body(): projected = lax.all_gather(own_proj, 'row', axis=0, tiled=True)]
    pmax x1 -> x0, blocking collectives: 48.2 us -> none  [body(): row_max = lax.pmax(row_max, 'col')]
    psum x1 -> x0, blocking collectives: 27 us -> none  [body(): lax.psum(denoms.astype(jnp.bfloat16), 'col').astype(jnp.float32)]
    all_gather x1 -> x0, blocking collectives: 24.6 us -> none  [body(): dst_logits = lax.all_gather(dst_local, 'col', axis=1, tiled=True)]
    dot_general x7 -> x0, matrix products: 20.3 us -> none  [the longest x1 9.89 us: body(): jnp.einsum('hsji,sjhk->sihk', weights, src_feats, preferred_element_type=...]
    unnamed x15 -> x19, local copies, waits for them, and re-layouts: 1.11 us -> 6.7 us
  transfers between devices with their start and end apart: 2 -> 0, of which waited for: 2 -> 0; matrix products, arithmetic and copies ran while one was open for 4% -> 0% of each run, Pallas kernels for 0% -> 0%
where the time goes in v2:
time: 68.8 us; the launch traced here: 68.5 us
  Pallas kernels  61 us (89%)
  local copies, waits for them, and re-layouts  6.7 us (10%)
  between operations  0.72 us (1%)
    pallas_call x1, Pallas kernels, scores(): pl.pallas_call(scores_kernel, out_shape=(jax.ShapeDtypeStruct((ROWS, OWN,...  37 us
    pallas_call x1, Pallas kernels, combine(): pl.pallas_call(combine_kernel, out_shape=jax.ShapeDtypeStruct((OWN, WIDTH...  19.3 us
    unnamed x19, local copies, waits for them, and re-layouts  6.7 us
    pallas_call x1, Pallas kernels, sums(): pl.pallas_call(sums_kernel, out_shape=(jax.ShapeDtypeStruct((DB, WIDTH, B...  4.75 us

profile of v2, /device:TPU:1, one launch (start us, length us, event | category | flops | bytes accessed | tf_op | source)
XLA Modules:
  0.0 68.5 jit_solution(7373133166956950443)
XLA Ops:
  0.0 0.0 copy-start.8
  0.7 0.0 copy-start
  0.7 1.0 %copy-done = s32[1,1,48,16,128]{4,3,2,1,0:T(8,128)S(1)} copy-done((s32[1,1,48,16,128]{4,3,2,1,0:T(8,128)S(1)}, s32[1,1,48,16,128]{4,3,2,1,0:T(8,128)}, u32[]{:S(2)}) %copy-start) | copy-done | bytes 393240
  1.7 0.0 copy-start.1
  1.7 0.9 %copy-done.1 = bf16[256,256]{1,0:T(8,128)(2,1)S(1)} copy-done((bf16[256,256]{1,0:T(8,128)(2,1)S(1)}, bf16[256,256]{1,0:T(8,128)(2,1)}, u32[]{:S(2)}) %copy-start.1) | copy-done | bytes 131096
  2.6 0.0 copy-start.2
  2.6 0.8 %copy-done.2 = bf16[1,64,256]{2,1,0:T(8,128)(2,1)S(1)} copy-done((bf16[1,64,256]{2,1,0:T(8,128)(2,1)S(1)}, bf16[1,64,256]{2,1,0:T(8,128)(2,1)}, u32[]{:S(2)}) %copy-start.2) | copy-done | bytes 32792
  3.3 0.0 copy-start.3
  3.3 0.8 %copy-done.3 = bf16[64,256]{1,0:T(8,128)(2,1)S(1)} copy-done((bf16[64,256]{1,0:T(8,128)(2,1)S(1)}, bf16[64,256]{1,0:T(8,128)(2,1)}, u32[]{:S(2)}) %copy-start.3) | copy-done | bytes 32792
  4.1 0.0 copy-start.4
  4.1 0.7 copy-done.4
  4.8 0.0 copy-start.5
  4.8 0.7 copy-done.5
  5.5 0.0 copy-start.6
  5.5 0.7 copy-done.6
  6.1 37.0 %scores.1 = (bf16[32,64,128]{2,1,0:T(8,128)(2,1)S(1)}, bf16[32,64,128]{2,1,0:T(8,128)(2,1)S(1)}, bf16[48,4,128,128]{3,2,1,0:T(8,128)(2,1)S(1)}, f32[48,4,8,128]{3,2,1,0:T(8,128)S(1)}, f32[8,8,128]{2,1,0:T(8,128)S(1)}) custom-call(bf16[64,256]{1,0:T(8,128)(2,1)S(1)} %bitcast.9, bf16[64,256]{1,0:T(8,128)(2,1)S(1)} %copy-done.3, ...), custom_call_target="tpu_custom_call" | custom-call | tf_op jit(solution)/shard_map/scores/pallas_call | solution.py:272
  43.1 0.0 copy-start.7
  43.1 0.6 copy-done.7
  43.7 4.7 %sums.1 = (bf16[8,256,128]{2,1,0:T(8,128)(2,1)S(1)}, f32[8,8,128]{2,1,0:T(8,128)S(1)}) custom-call(s32[1,48]{1,0:T(1,128)S(1)} %bitcast.11, bf16[2048,128]{1,0:T(8,128)(2,1)S(1)} %bitcast.6, bf16[2048,128]{1,0:T(8,128)(2,1)S(1)} %bitcast.7, bf16[48,4,128,128]{3,2,1,0:T(8,128)(2,1)S(1)} %get-tuple-element.14.weights_ref, ...), custom_call_target="tpu_custom_call" | custom-call | tf_op jit(solution)/shard_map/sums/pallas_call | solution.py:345
  48.5 0.0 copy-done.8
  48.5 19.3 %combine.1 = bf16[64,256]{1,0:T(8,128)(2,1)S(1)} custom-call(bf16[8,256,128]{2,1,0:T(8,128)(2,1)S(1)} %get-tuple-element.17.accum_ref, f32[8,8,128]{2,1,0:T(8,128)S(1)} %get-tuple-element.18.stats_ref, f32[1,256]{1,0:T(1,128)S(1)} %bitcast.12), custom_call_target="tpu_custom_call" | custom-call | tf_op jit(solution)/shard_map/combine/pallas_call | solution.py:478
  67.8 0.6 copy.12
Async XLA Ops:
  0.0 48.5 %copy-start.8 = (f32[256]{0:T(256)S(1)}, f32[256]{0:T(256)}, u32[]{:S(2)}) copy-start(f32[256]{0:T(256)} %param.14) | copy-start | bytes 3076
  0.7 1.0 %copy-start = (s32[1,1,48,16,128]{4,3,2,1,0:T(8,128)S(1)}, s32[1,1,48,16,128]{4,3,2,1,0:T(8,128)}, u32[]{:S(2)}) copy-start(s32[1,1,48,16,128]{4,3,2,1,0:T(8,128)} %param.17) | copy-start | bytes 1179652
  1.7 0.9 %copy-start.1 = (bf16[256,256]{1,0:T(8,128)(2,1)S(1)}, bf16[256,256]{1,0:T(8,128)(2,1)}, u32[]{:S(2)}) copy-start(bf16[256,256]{1,0:T(8,128)(2,1)} %weight_hbm.1) | copy-start | bytes 393220
  2.6 0.8 %copy-start.2 = (bf16[1,64,256]{2,1,0:T(8,128)(2,1)S(1)}, bf16[1,64,256]{2,1,0:T(8,128)(2,1)}, u32[]{:S(2)}) copy-start(bf16[1,64,256]{2,1,0:T(8,128)(2,1)} %param.9) | copy-start | bytes 98308
  3.3 0.8 %copy-start.3 = (bf16[64,256]{1,0:T(8,128)(2,1)S(1)}, bf16[64,256]{1,0:T(8,128)(2,1)}, u32[]{:S(2)}) copy-start(bf16[64,256]{1,0:T(8,128)(2,1)} %tgt_hbm.1) | copy-start | bytes 98308
  4.1 0.7 copy-start.4
  4.8 0.7 copy-start.5
  5.5 0.7 copy-start.6
  43.1 0.7 copy-start.7

commit v3 on v0

v3 whole, which is shorter than its diff:
```python
import jax
import jax.numpy as jnp
from jax import lax
from jax.experimental import pallas as pl
from jax.experimental.pallas import tpu as pltpu
from jax.sharding import PartitionSpec as P

BLK = 128
SB = 16
DB = 8
SLOTS = 48
HEADS = 4
HD = 64
WIDTH = 256
ROWS = 32
COLS = 16
XS = 4
YS = 8
ZS = 8
OWN = 64

very_low = -1e30
no_edge = -3e38
slope = 0.2
MESH = pl.DeviceIdType.MESH
by_columns = (((1,), (1,)), ((), ()))


def in_three(x):
    high = x.astype(jnp.bfloat16)
    rest = x - high.astype(jnp.float32)
    middle = rest.astype(jnp.bfloat16)
    low = (rest - middle.astype(jnp.float32)).astype(jnp.bfloat16)
    return low, middle, high


def leaky(x):
    return jnp.maximum(x, slope * x)


def loop(first, last, step):
    def one(i, _):
        step(i)
        return 0

    lax.fori_loop(first, last, one, 0)


def in_half(rows, position):
    twice = jnp.concatenate([rows, rows], axis=1)
    half = lax.broadcasted_iota(jnp.int32, (HEADS, BLK), 1) // OWN
    return jnp.where(half == lax.rem(position, 2), twice[:HEADS], 0.0)


def flat_scores(ref):
    return jnp.concatenate([ref[h : h + 1, :] for h in range(HEADS)], axis=1)


def layer_kernel(
    src_hbm, tgt_hbm, weight_hbm, source_hbm, target_hbm, bias_hbm, slots_hbm, live_hbm, bits_hbm,
    out_ref,
    src_ref, tgt_ref, weight_ref, source_ref, target_ref, bias_ref, slots_ref, live_ref, bits_ref,
    feats, src_rows, dst_half, dst, place_rows, places, everyone, spread, tops, maxima, turned,
    even, odd, slot_sums, products, accum, sent, stats, twin_sent, twin_stats,
    joint, joint_stats, got, got_stats, half_ref, twin_half,
    local, send_ay, recv_ay, send_ax, recv_ax, send_b, recv_b, send_y, recv_y, send_x, recv_x,
    send_p, recv_p, send_j, recv_j, send_k, recv_k, send_one, recv_one,
):
    row, col = lax.axis_index("row"), lax.axis_index("col")
    x, y = lax.rem(row, XS), row // XS
    z, core = col // 2, lax.rem(col, 2)
    twin = (row, col + 1 - 2 * core)
    pairs = (
        (weight_hbm, weight_ref), (src_hbm, src_ref), (source_hbm, source_ref), (tgt_hbm, tgt_ref),
        (target_hbm, target_ref), (slots_hbm, slots_ref), (live_hbm, live_ref), (bits_hbm, bits_ref),
        (bias_hbm, bias_ref),
    )
    loads = [pltpu.make_async_copy(a, b, local.at[i]) for i, (a, b) in enumerate(pairs)]
    for load in loads:
        load.start()

    def at_x(d):
        return (y * XS + lax.rem(x + d, XS), col)

    def at_y(d):
        return (lax.rem(y + d, YS) * XS + x, col)

    def at_z(d):
        return (row, lax.rem(z + d, ZS) * 2 + core)

    barrier = pltpu.get_barrier_semaphore()
    for d in range(1, YS):
        pl.semaphore_signal(barrier, inc=1, device_id=at_y(d), device_id_type=MESH)
    for d in range(1, XS):
        pl.semaphore_signal(barrier, inc=1, device_id=at_x(d), device_id_type=MESH)
    for d in range(1, ZS):
        pl.semaphore_signal(barrier, inc=1, device_id=at_z(d), device_id_type=MESH)
    pl.semaphore_signal(barrier, inc=1, device_id=twin, device_id_type=MESH)

    def send(source, target, semaphores, device):
        return pltpu.make_async_remote_copy(
            src_ref=source, dst_ref=target, send_sem=semaphores[0], recv_sem=semaphores[1],
            device_id=device, device_id_type=MESH,
        )

    def logits_y(d):
        return send(src_rows.at[x, y], src_rows.at[x, y], (send_ay.at[d], recv_ay.at[d]), at_y(d))

    def logits_x(d):
        return send(src_rows.at[x], src_rows.at[x], (send_ax.at[d], recv_ax.at[d]), at_x(d))

    def feats_y(d):
        return send(feats.at[row], feats.at[row], (send_y.at[d], recv_y.at[d]), at_y(d))

    def feats_x(d, e):
        block = lax.rem(y - d + YS, YS) * XS + x
        return send(feats.at[block], feats.at[block], (send_x.at[d, e], recv_x.at[d, e]), at_x(e))

    def target_pair():
        return send(dst_half.at[0], dst_half.at[1], (send_one.at[0], recv_one.at[0]), twin)

    def target_z(d):
        return send(dst.at[z], dst.at[z], (send_b.at[d], recv_b.at[d]), at_z(d))

    def stats_pair():
        return send(stats, twin_stats, (send_one.at[1], recv_one.at[1]), twin)

    def sums_pair(d):
        theirs = pl.ds(pl.multiple_of((1 - core) * BLK, BLK), BLK)
        return send(sent.at[d, theirs], twin_sent.at[d], (send_p.at[d], recv_p.at[d]), twin)

    def sums_z(d):
        return send(joint.at[lax.rem(z + d, ZS)], got.at[z], (send_j.at[d], recv_j.at[d]), at_z(d))

    def stats_z(d):
        return send(joint_stats.at[lax.rem(z + d, ZS)], got_stats.at[z], (send_k.at[d], recv_k.at[d]), at_z(d))

    def result_pair():
        return send(half_ref, twin_half, (send_one.at[2], recv_one.at[2]), twin)

    for load in loads[:3]:
        load.wait()
    own = jnp.dot(src_ref[...], weight_ref[...], preferred_element_type=jnp.float32).astype(jnp.bfloat16)
    feats[row] = own
    head_of = lax.broadcasted_iota(jnp.int32, (8, WIDTH), 1) // HD
    pick = head_of == lax.broadcasted_iota(jnp.int32, (8, WIDTH), 0)
    parts = jnp.concatenate(in_three(jnp.where(pick, flat_scores(source_ref), 0.0)), axis=0)
    logits = lax.dot_general(parts, own, by_columns, preferred_element_type=jnp.float32)
    src_rows[x, y] = in_half(logits[0:8] + logits[8:16] + logits[16:24], row)
    pl.semaphore_wait(barrier, XS + YS + ZS - 2)

    far_first = (4, 3, 5, 2, 6, 1, 7)
    near_first = (1, 7, 2, 6, 3, 5, 4)
    for d in far_first:
        logits_y(d).start()
    for d in far_first:
        feats_y(d).start()
    for e in range(1, XS):
        feats_x(0, e).start()

    for load in loads[3:5]:
        load.wait()
    product = jnp.dot(tgt_ref[...], weight_ref[...], preferred_element_type=jnp.float32) * flat_scores(target_ref)
    ones = pick.astype(jnp.bfloat16)
    logits = [lax.dot_general(ones, part, by_columns, preferred_element_type=jnp.float32) for part in in_three(product)]
    dst_half[0] = in_half(logits[0] + logits[1] + logits[2], col)
    target_pair().start()

    for load in loads[5:]:
        load.wait()
    live = live_ref[0, 0]
    lane = lax.broadcasted_iota(jnp.int32, (1, BLK), 1)

    def put(slot, table):
        name = slots_ref[0, slot] + BLK * jnp.clip(slot + 1 - live, 0, 1)
        return jnp.where(lane == jnp.full((1, BLK), name, jnp.int32), slot, table)

    place_rows[...] = lax.fori_loop(0, SLOTS, put, jnp.full((1, BLK), SLOTS, jnp.int32), unroll=8)
    table = pltpu.make_async_copy(place_rows, places, local.at[9])
    table.start()
    everyone[...] = jnp.zeros(everyone.shape, jnp.float32)
    tops[SLOTS] = jnp.full((HEADS, 8, BLK), no_edge, jnp.float32)
    slot_sums[SLOTS] = jnp.zeros((HEADS, 8, BLK), jnp.float32)
    products[SLOTS] = jnp.zeros((WIDTH, BLK), jnp.float32)
    odd[...] = jnp.zeros(odd.shape, jnp.bfloat16)
    target_pair().wait_recv()
    dst[z] = dst_half[0] + dst_half[1]
    for d in range(1, ZS):
        target_z(d).start()

    for d in near_first:
        logits_y(d).wait_recv()
    for e in range(1, XS):
        logits_x(e).start()
    for d in near_first:
        feats_y(d).wait_recv()
        for e in range(1, XS):
            feats_x(d, e).start()
    for e in range(1, XS):
        logits_x(e).wait_recv()
    for s in range(SB):
        here, pair = s // 2, (s % 2) * 2
        everyone[8 * s : 8 * s + HEADS, :] = src_rows[pair, here] + src_rows[pair + 1, here]
    columns = everyone[...].T
    for s in range(SB):
        for h in range(HEADS):
            spread[h, s] = jnp.broadcast_to(columns[:, 8 * s + h : 8 * s + h + 1], (BLK, BLK))

    bit = jnp.left_shift(1, lax.broadcasted_iota(jnp.int32, (8, BLK), 0))

    def edges(slot, w):
        words = bits_ref[slot, pl.ds(w, 1), :]
        return (jnp.broadcast_to(words, (8, BLK)) & bit) != 0

    def slot_max(slot):
        s = slots_ref[0, slot] & (SB - 1)
        top = [jnp.full((8, BLK), no_edge, jnp.float32)] * HEADS
        for w in range(BLK // 8):
            mask = edges(slot, w)
            for h in range(HEADS):
                top[h] = jnp.maximum(top[h], jnp.where(mask, spread[h, s, 8 * w : 8 * w + 8, :], no_edge))
        for h in range(HEADS):
            tops[slot, h] = top[h]

    loop(0, SLOTS, slot_max)
    table.wait()
    for d in range(1, ZS):
        target_z(d).wait_recv()

    def block_max(d):
        best = [tops[places[0, d * SB], h] for h in range(HEADS)]
        for k in range(1, SB):
            slot = places[0, d * SB + k]
            best = [jnp.maximum(best[h], tops[slot, h]) for h in range(HEADS)]
        for h in range(HEADS):
            top = jnp.max(best[h], axis=0, keepdims=True)
            maxima[d, h : h + 1, :] = jnp.where(top > -1e38, leaky(top + dst[d, h : h + 1, :]), very_low)

    loop(0, DB, block_max)

    for d in range(YS):
        for e in range(1, XS):
            feats_x(d, e).wait_recv()
    eye = (
        lax.broadcasted_iota(jnp.int32, (WIDTH, WIDTH), 0) == lax.broadcasted_iota(jnp.int32, (WIDTH, WIDTH), 1)
    ).astype(jnp.bfloat16)

    def turn(s):
        block = jnp.concatenate([feats[2 * s], feats[2 * s + 1]], axis=0)
        turned[s] = lax.dot_general(eye, block, by_columns, preferred_element_type=jnp.float32).astype(jnp.bfloat16)

    loop(0, SB, turn)

    def slot_weights(slot, weights):
        place = slots_ref[0, slot]
        d, s = jnp.right_shift(place, 4), place & (SB - 1)
        sums = [jnp.zeros((8, BLK), jnp.float32)] * HEADS
        b = [jnp.broadcast_to(dst[d, h : h + 1, :], (8, BLK)) for h in range(HEADS)]
        m = [jnp.broadcast_to(maxima[d, h : h + 1, :], (8, BLK)) for h in range(HEADS)]
        for w in range(0, BLK // 8, 2):
            masks = [edges(slot, w), edges(slot, w + 1)]
            for h in range(HEADS):
                pair = []
                for half in range(2):
                    from_src = spread[h, s, 8 * (w + half) : 8 * (w + half) + 8, :]
                    score = leaky(from_src + b[h]) - m[h]
                    numer = jnp.where(masks[half], jnp.exp(score), 0.0)
                    sums[h] = sums[h] + numer
                    pair.append(numer)
                weights[h, 8 * w : 8 * w + 16, :] = jnp.concatenate(pair, axis=0).astype(jnp.bfloat16)
        for h in range(HEADS):
            slot_sums[slot, h] = sums[h]

    def slot_product(slot, weights):
        s = slots_ref[0, slot] & (SB - 1)
        for h in range(HEADS):
            rows = slice(h * HD, (h + 1) * HD)
            products[slot, rows, :] = jnp.dot(turned[s, rows, :], weights[h], preferred_element_type=jnp.float32)

    def two_slots(i):
        slot_product(jnp.maximum(2 * i - 1, 0), odd)
        slot_weights(2 * i, even)
        slot_product(2 * i, even)
        slot_weights(2 * i + 1, odd)

    loop(0, SLOTS // 2, two_slots)
    slot_product(SLOTS - 1, odd)

    def block_stats(d):
        total = [slot_sums[places[0, d * SB], h] for h in range(HEADS)]
        for k in range(1, SB):
            slot = places[0, d * SB + k]
            total = [total[h] + slot_sums[slot, h] for h in range(HEADS)]
        rows = [maxima[d]] + [jnp.sum(total[h], axis=0, keepdims=True) for h in range(HEADS)]
        stats[d] = jnp.concatenate(rows, axis=0)

    loop(0, DB, block_stats)
    stats_pair().start()
    order = (4, 3, 5, 2, 6, 1, 7, 0)
    for o in order:
        d = lax.rem(z + o, ZS)

        def add(k, total):
            for i in range(4):
                total = total + products[places[0, d * SB + 4 * k + i]]
            return total

        total = lax.fori_loop(0, SB // 4, add, jnp.zeros((WIDTH, BLK), jnp.float32))
        accum[d] = total
        sent[d] = total.astype(jnp.bfloat16)
        sums_pair(d).start()
    stats_pair().wait_recv()

    def own_heads(tile):
        return jnp.where(core == 0, tile[0:2], tile[2:4]), jnp.where(core == 0, tile[4:6], tile[6:8])

    for o in order:
        d = lax.rem(z + o, ZS)
        m0, s0 = own_heads(stats[d])
        m1, s1 = own_heads(twin_stats[d])
        m = jnp.maximum(m0, m1)
        f0, f1 = jnp.exp(m0 - m), jnp.exp(m1 - m)
        tile = jnp.concatenate([m, s0 * f0 + s1 * f1, m, m], axis=0)
        sums_pair(d).wait_recv()
        mixed = []
        for h in range(2):
            rows = pl.ds(pl.multiple_of(core * BLK + h * HD, HD), HD)
            twin_part = twin_sent[d, h * HD : (h + 1) * HD, :].astype(jnp.float32)
            mixed.append(accum[d, rows, :] * f0[h : h + 1] + twin_part * f1[h : h + 1])
        mixed = jnp.concatenate(mixed, axis=0).astype(jnp.bfloat16)
        if o:
            joint_stats[d] = tile
            joint[d] = mixed
            stats_z(o).start()
            sums_z(o).start()
        else:
            got_stats[z] = tile
            got[z] = mixed

    for d in range(1, ZS):
        stats_z(d).wait_recv()
    every = got_stats[...]
    near = every[:, 0:2, :]
    factor = jnp.exp(near - jnp.max(near, axis=0, keepdims=True))
    denoms = jnp.sum(factor * every[:, 2:4, :], axis=0, keepdims=True)
    factor = factor / jnp.maximum(denoms, 1.0)
    for d in range(1, ZS):
        sums_z(d).wait_recv()
    parts = []
    for h in range(2):
        part = jnp.zeros((HD, BLK), jnp.float32)
        for c in range(ZS):
            part = part + factor[c, h : h + 1, :] * got[c, h * HD : (h + 1) * HD, :].astype(jnp.float32)
        parts.append(part)
    bias = jnp.where(core == 0, bias_ref[:, :BLK], bias_ref[:, BLK:])
    blended = jnp.concatenate(parts, axis=0).T + bias
    result = jnp.where(blended > 0, blended, jnp.exp(jnp.minimum(blended, 0.0)) - 1.0).astype(jnp.bfloat16)
    half_ref[...] = jnp.where(core == 0, result[OWN:], result[:OWN])
    result_pair().start()
    out_ref[:, pl.ds(pl.multiple_of(core * BLK, BLK), BLK)] = jnp.where(core == 0, result[:OWN], result[OWN:])

    for d in range(1, YS):
        logits_y(d).wait_send()
        feats_y(d).wait_send()
    for e in range(1, XS):
        logits_x(e).wait_send()
        for d in range(YS):
            feats_x(d, e).wait_send()
    target_pair().wait_send()
    stats_pair().wait_send()
    for d in range(1, ZS):
        target_z(d).wait_send()
        stats_z(d).wait_send()
        sums_z(d).wait_send()
    loop(0, ZS, lambda d: sums_pair(d).wait_send())
    result_pair().wait()
    out_ref[:, pl.ds(pl.multiple_of((1 - core) * BLK, BLK), BLK)] = twin_half[...]


def layer(source, target, weight, score_source, score_target, bias, slots, live, bits):
    dma = pltpu.SemaphoreType.DMA
    vmem = pltpu.VMEM
    f32, bf16 = jnp.float32, jnp.bfloat16
    return pl.pallas_call(
        layer_kernel,
        out_shape=jax.ShapeDtypeStruct((OWN, WIDTH), bf16),
        in_specs=[pl.BlockSpec(memory_space=pltpu.HBM)] * 9,
        out_specs=pl.BlockSpec(memory_space=pltpu.VMEM),
        scratch_shapes=[
            vmem((OWN, WIDTH), bf16),
            vmem((OWN, WIDTH), bf16),
            vmem((WIDTH, WIDTH), bf16),
            vmem((HEADS, HD), f32),
            vmem((HEADS, HD), f32),
            vmem((1, WIDTH), f32),
            pltpu.SMEM((1, SLOTS), jnp.int32),
            pltpu.SMEM((1, 1), jnp.int32),
            vmem((SLOTS, BLK // 8, BLK), jnp.int32),
            vmem((ROWS, OWN, WIDTH), bf16),
            vmem((XS, YS, HEADS, BLK), f32),
            vmem((2, HEADS, BLK), f32),
            vmem((DB, HEADS, BLK), f32),
            vmem((1, BLK), jnp.int32),
            pltpu.SMEM((1, BLK), jnp.int32),
            vmem((BLK, BLK), f32),
            vmem((HEADS, SB, BLK, BLK), f32),
            vmem((SLOTS + 1, HEADS, 8, BLK), f32),
            vmem((DB, HEADS, BLK), f32),
            vmem((SB, WIDTH, BLK), bf16),
            vmem((HEADS, BLK, BLK), bf16),
            vmem((HEADS, BLK, BLK), bf16),
            vmem((SLOTS + 1, HEADS, 8, BLK), f32),
            vmem((SLOTS + 1, WIDTH, BLK), f32),
            vmem((DB, WIDTH, BLK), f32),
            vmem((DB, WIDTH, BLK), bf16),
            vmem((DB, 8, BLK), f32),
            vmem((DB, BLK, BLK), bf16),
            vmem((DB, 8, BLK), f32),
            vmem((DB, BLK, BLK), bf16),
            vmem((DB, 8, BLK), f32),
            vmem((DB, BLK, BLK), bf16),
            vmem((DB, 8, BLK), f32),
            vmem((OWN, BLK), bf16),
            vmem((OWN, BLK), bf16),
            dma((10,)),
            dma((YS,)), dma((YS,)),
            dma((XS,)), dma((XS,)),
            dma((ZS,)), dma((ZS,)),
            dma((YS,)), dma((YS,)),
            dma((YS, XS)), dma((YS, XS)),
            dma((ZS,)), dma((ZS,)),
            dma((ZS,)), dma((ZS,)),
            dma((ZS,)), dma((ZS,)),
            dma((3,)), dma((3,)),
        ],
        compiler_params=pltpu.CompilerParams(collective_id=0, has_side_effects=True, vmem_limit_bytes=60 << 20),
        name="layer",
    )(source, target, weight, score_source, score_target, bias, slots, live, bits)


def body(
    source_features, target_features, weight, score_source, score_target, out_bias,
    block_list, block_count, edge_bits,
):
    return layer(
        source_features[0], target_features, weight, score_source, score_target, out_bias.reshape(1, WIDTH),
        block_list[0], block_count, edge_bits[0, 0],
    )


def solution(mesh):
    placed = (
        P("col", "row", None),
        P(("row", "col"), None),
        P(),
        P(),
        P(),
        P(),
        P("row", "col", None),
        P("row", "col"),
        P("row", "col", None, None, None),
    )
    return jax.shard_map(
        body, mesh=mesh, in_specs=placed, out_specs=P(("row", "col"), None), check_vma=False
    )
```

time: 297 us -> 62.1 us (0.21)
  waiting for transfers between devices: 136 us -> 0 us
  blocking collectives: 99.8 us -> 0 us
  Pallas kernels: 0 us -> 59.9 us
  matrix products: 20.3 us -> 0 us
  other arithmetic: 15.7 us -> 0 us
  between operations: 14.3 us -> 0.66 us
  local copies, waits for them, and re-layouts: 10.9 us -> 1.38 us
    psum x1 -> x0, waiting for transfers between devices: 83 us -> none  [body(): lax.psum(accum.astype(jnp.bfloat16), 'col').astype(jnp.float32)]
    pallas_call x0 -> x1, Pallas kernels: none -> 59.9 us  [layer(): pl.pallas_call(layer_kernel, out_shape=jax.ShapeDtypeStruct((OWN, WIDTH),...]
    all_gather x1 -> x0, waiting for transfers between devices: 52.5 us -> none  [body(): projected = lax.all_gather(own_proj, 'row', axis=0, tiled=True)]
    pmax x1 -> x0, blocking collectives: 48.2 us -> none  [body(): row_max = lax.pmax(row_max, 'col')]
    psum x1 -> x0, blocking collectives: 27 us -> none  [body(): lax.psum(denoms.astype(jnp.bfloat16), 'col').astype(jnp.float32)]
    all_gather x1 -> x0, blocking collectives: 24.6 us -> none  [body(): dst_logits = lax.all_gather(dst_local, 'col', axis=1, tiled=True)]
    dot_general x7 -> x0, matrix products: 20.3 us -> none  [the longest x1 9.89 us: body(): jnp.einsum('hsji,sjhk->sihk', weights, src_feats, preferred_element_type=...]
    reduce_sum x1 -> x0, other arithmetic: 5.5 us -> none  [body(): slot_denoms = jnp.sum(numer, axis=2)]
  transfers between devices with their start and end apart: 2 -> 0, of which waited for: 2 -> 0; matrix products, arithmetic and copies ran while one was open for 4% -> 0% of each run, Pallas kernels for 0% -> 0%
where the time goes in v3:
time: 62.1 us; the launch traced here: 61.9 us
  Pallas kernels  59.9 us (96%)
  local copies, waits for them, and re-layouts  1.38 us (2%)
  between operations  0.66 us (1%)
    pallas_call x1, Pallas kernels, layer(): pl.pallas_call(layer_kernel, out_shape=jax.ShapeDtypeStruct((OWN, WIDTH),...  59.9 us
    unnamed x1, local copies, waits for them, and re-layouts  1.38 us

profile of v3, /device:TPU:1, one launch (start us, length us, event | category | flops | bytes accessed | tf_op | source)
XLA Modules:
  0.0 61.9 jit_solution(5310723668372922093)
XLA Ops:
  0.7 59.9 %layer.1 = bf16[64,256]{1,0:T(8,128)(2,1)} custom-call(bf16[64,256]{1,0:T(8,128)(2,1)} %bitcast.5, bf16[64,256]{1,0:T(8,128)(2,1)} %tgt_hbm.1, bf16[256,256]{1,0:T(8,128)(2,1)} %weight_hbm.1, f32[4,64]{1,0:T(4,128)} %source_hbm.1, f32[4,64]{1,0:T(4,128)} %target_hbm.1, f32[1,256]{1,0:T(1,128)} %bitcast.6, s32[1,48]{1,0:T(1,128)} %bitcast.7, ...), custom_call_target="tpu_custom_call" | custom-call | tf_op jit(solution)/shard_map/layer/pallas_call | solution.py:384
  60.6 1.4 %copy.12 = bf16[64,256]{1,0:T(8,128)(2,1)} copy(bf16[64,256]{1,0:T(8,128)(2,1)} %layer.1) | data formatting | bytes 65536

commit v4 on v3

--- a/solution.py
+++ b/solution.py
@@ -22,6 +22,7 @@
 very_low = -1e30
 no_edge = -3e38
 slope = 0.2
+log2e = 1.4426950408889634
 MESH = pl.DeviceIdType.MESH
 by_columns = (((1,), (1,)), ((), ()))
 
@@ -38,12 +39,12 @@
     return jnp.maximum(x, slope * x)
 
 
-def loop(first, last, step):
+def loop(first, last, step, unroll=1):
     def one(i, _):
         step(i)
         return 0
 
-    lax.fori_loop(first, last, one, 0)
+    lax.fori_loop(first, last, one, 0, unroll=unroll)
 
 
 def in_half(rows, position):
@@ -61,7 +62,7 @@
     out_ref,
     src_ref, tgt_ref, weight_ref, source_ref, target_ref, bias_ref, slots_ref, live_ref, bits_ref,
     feats, src_rows, dst_half, dst, place_rows, places, everyone, spread, tops, maxima, turned,
-    even, odd, slot_sums, products, accum, sent, stats, twin_sent, twin_stats,
+    weights, slot_sums, products, accum, sent, stats, twin_sent, twin_stats,
     joint, joint_stats, got, got_stats, half_ref, twin_half,
     local, send_ay, recv_ay, send_ax, recv_ax, send_b, recv_b, send_y, recv_y, send_x, recv_x,
     send_p, recv_p, send_j, recv_j, send_k, recv_k, send_one, recv_one,
@@ -146,24 +147,24 @@
     pick = head_of == lax.broadcasted_iota(jnp.int32, (8, WIDTH), 0)
     parts = jnp.concatenate(in_three(jnp.where(pick, flat_scores(source_ref), 0.0)), axis=0)
     logits = lax.dot_general(parts, own, by_columns, preferred_element_type=jnp.float32)
-    src_rows[x, y] = in_half(logits[0:8] + logits[8:16] + logits[16:24], row)
+    src_rows[x, y] = in_half((logits[0:8] + logits[8:16] + logits[16:24]) * log2e, row)
     pl.semaphore_wait(barrier, XS + YS + ZS - 2)
 
     far_first = (4, 3, 5, 2, 6, 1, 7)
     near_first = (1, 7, 2, 6, 3, 5, 4)
     for d in far_first:
         logits_y(d).start()
-    for d in far_first:
+    for e in (2, 1, 3):
+        feats_x(0, e).start()
+    for d in near_first:
         feats_y(d).start()
-    for e in range(1, XS):
-        feats_x(0, e).start()
 
     for load in loads[3:5]:
         load.wait()
     product = jnp.dot(tgt_ref[...], weight_ref[...], preferred_element_type=jnp.float32) * flat_scores(target_ref)
     ones = pick.astype(jnp.bfloat16)
     logits = [lax.dot_general(ones, part, by_columns, preferred_element_type=jnp.float32) for part in in_three(product)]
-    dst_half[0] = in_half(logits[0] + logits[1] + logits[2], col)
+    dst_half[0] = in_half((logits[0] + logits[1] + logits[2]) * log2e, col)
     target_pair().start()
 
     for load in loads[5:]:
@@ -182,7 +183,6 @@
     tops[SLOTS] = jnp.full((HEADS, 8, BLK), no_edge, jnp.float32)
     slot_sums[SLOTS] = jnp.zeros((HEADS, 8, BLK), jnp.float32)
     products[SLOTS] = jnp.zeros((WIDTH, BLK), jnp.float32)
-    odd[...] = jnp.zeros(odd.shape, jnp.bfloat16)
     target_pair().wait_recv()
     dst[z] = dst_half[0] + dst_half[1]
     for d in range(1, ZS):
@@ -194,7 +194,7 @@
         logits_x(e).start()
     for d in near_first:
         feats_y(d).wait_recv()
-        for e in range(1, XS):
+        for e in (2, 1, 3):
             feats_x(d, e).start()
     for e in range(1, XS):
         logits_x(e).wait_recv()
@@ -209,8 +209,7 @@
     bit = jnp.left_shift(1, lax.broadcasted_iota(jnp.int32, (8, BLK), 0))
 
     def edges(slot, w):
-        words = bits_ref[slot, pl.ds(w, 1), :]
-        return (jnp.broadcast_to(words, (8, BLK)) & bit) != 0
+        return (bits_ref[slot, pl.ds(w, 8, stride=0), :] & bit) != 0
 
     def slot_max(slot):
         s = slots_ref[0, slot] & (SB - 1)
@@ -222,7 +221,7 @@
         for h in range(HEADS):
             tops[slot, h] = top[h]
 
-    loop(0, SLOTS, slot_max)
+    loop(0, SLOTS, slot_max, 2)
     table.wait()
     for d in range(1, ZS):
         target_z(d).wait_recv()
@@ -238,20 +237,7 @@
 
     loop(0, DB, block_max)
 
-    for d in range(YS):
-        for e in range(1, XS):
-            feats_x(d, e).wait_recv()
-    eye = (
-        lax.broadcasted_iota(jnp.int32, (WIDTH, WIDTH), 0) == lax.broadcasted_iota(jnp.int32, (WIDTH, WIDTH), 1)
-    ).astype(jnp.bfloat16)
-
-    def turn(s):
-        block = jnp.concatenate([feats[2 * s], feats[2 * s + 1]], axis=0)
-        turned[s] = lax.dot_general(eye, block, by_columns, preferred_element_type=jnp.float32).astype(jnp.bfloat16)
-
-    loop(0, SB, turn)
-
-    def slot_weights(slot, weights):
+    def slot_weights(slot):
         place = slots_ref[0, slot]
         d, s = jnp.right_shift(place, 4), place & (SB - 1)
         sums = [jnp.zeros((8, BLK), jnp.float32)] * HEADS
@@ -264,27 +250,14 @@
                 for half in range(2):
                     from_src = spread[h, s, 8 * (w + half) : 8 * (w + half) + 8, :]
                     score = leaky(from_src + b[h]) - m[h]
-                    numer = jnp.where(masks[half], jnp.exp(score), 0.0)
+                    numer = jnp.where(masks[half], jnp.exp2(score), 0.0)
                     sums[h] = sums[h] + numer
                     pair.append(numer)
-                weights[h, 8 * w : 8 * w + 16, :] = jnp.concatenate(pair, axis=0).astype(jnp.bfloat16)
+                weights[slot, h, 8 * w : 8 * w + 16, :] = jnp.concatenate(pair, axis=0).astype(jnp.bfloat16)
         for h in range(HEADS):
             slot_sums[slot, h] = sums[h]
 
-    def slot_product(slot, weights):
-        s = slots_ref[0, slot] & (SB - 1)
-        for h in range(HEADS):
-            rows = slice(h * HD, (h + 1) * HD)
-            products[slot, rows, :] = jnp.dot(turned[s, rows, :], weights[h], preferred_element_type=jnp.float32)
-
-    def two_slots(i):
-        slot_product(jnp.maximum(2 * i - 1, 0), odd)
-        slot_weights(2 * i, even)
-        slot_product(2 * i, even)
-        slot_weights(2 * i + 1, odd)
-
-    loop(0, SLOTS // 2, two_slots)
-    slot_product(SLOTS - 1, odd)
+    loop(0, SLOTS, slot_weights, 2)
 
     def block_stats(d):
         total = [slot_sums[places[0, d * SB], h] for h in range(HEADS)]
@@ -296,6 +269,29 @@
 
     loop(0, DB, block_stats)
     stats_pair().start()
+    for d in range(YS):
+        for e in range(1, XS):
+            feats_x(d, e).wait_recv()
+    eye = (
+        lax.broadcasted_iota(jnp.int32, (WIDTH, WIDTH), 0) == lax.broadcasted_iota(jnp.int32, (WIDTH, WIDTH), 1)
+    ).astype(jnp.bfloat16)
+
+    def turn(s):
+        block = jnp.concatenate([feats[2 * s], feats[2 * s + 1]], axis=0)
+        turned[s] = lax.dot_general(eye, block, by_columns, preferred_element_type=jnp.float32).astype(jnp.bfloat16)
+
+    for s in range(SB):
+        turn(s)
+
+    def slot_product(slot):
+        s = slots_ref[0, slot] & (SB - 1)
+        parts = [
+            jnp.dot(turned[s, h * HD : (h + 1) * HD, :], weights[slot, h], preferred_element_type=jnp.float32)
+            for h in range(HEADS)
+        ]
+        products[slot] = jnp.concatenate(parts, axis=0)
+
+    loop(0, SLOTS, slot_product, 16)
     order = (4, 3, 5, 2, 6, 1, 7, 0)
     for o in order:
         d = lax.rem(z + o, ZS)
@@ -319,7 +315,7 @@
         m0, s0 = own_heads(stats[d])
         m1, s1 = own_heads(twin_stats[d])
         m = jnp.maximum(m0, m1)
-        f0, f1 = jnp.exp(m0 - m), jnp.exp(m1 - m)
+        f0, f1 = jnp.exp2(m0 - m), jnp.exp2(m1 - m)
         tile = jnp.concatenate([m, s0 * f0 + s1 * f1, m, m], axis=0)
         sums_pair(d).wait_recv()
         mixed = []
@@ -341,7 +337,7 @@
         stats_z(d).wait_recv()
     every = got_stats[...]
     near = every[:, 0:2, :]
-    factor = jnp.exp(near - jnp.max(near, axis=0, keepdims=True))
+    factor = jnp.exp2(near - jnp.max(near, axis=0, keepdims=True))
     denoms = jnp.sum(factor * every[:, 2:4, :], axis=0, keepdims=True)
     factor = factor / jnp.maximum(denoms, 1.0)
     for d in range(1, ZS):
@@ -364,7 +360,8 @@
         feats_y(d).wait_send()
     for e in range(1, XS):
         logits_x(e).wait_send()
-        for d in range(YS):
+    for d in range(YS):
+        for e in range(1, XS):
             feats_x(d, e).wait_send()
     target_pair().wait_send()
     stats_pair().wait_send()
@@ -407,8 +404,7 @@
             vmem((SLOTS + 1, HEADS, 8, BLK), f32),
             vmem((DB, HEADS, BLK), f32),
             vmem((SB, WIDTH, BLK), bf16),
-            vmem((HEADS, BLK, BLK), bf16),
-            vmem((HEADS, BLK, BLK), bf16),
+            vmem((SLOTS, HEADS, BLK, BLK), bf16),
             vmem((SLOTS + 1, HEADS, 8, BLK), f32),
             vmem((SLOTS + 1, WIDTH, BLK), f32),
             vmem((DB, WIDTH, BLK), f32),

time: 62.1 us -> 50.2 us (0.81)
  Pallas kernels: 59.9 us -> 48 us
    pallas_call x1, Pallas kernels: 59.9 us -> 48 us  [layer(): pl.pallas_call(layer_kernel, out_shape=jax.ShapeDtypeStruct((OWN, WIDTH),...]
where the time goes in v4:
time: 50.2 us; the launch traced here: 50 us
  Pallas kernels  48 us (96%)
  local copies, waits for them, and re-layouts  1.38 us (3%)
  between operations  0.66 us (1%)
    pallas_call x1, Pallas kernels, layer(): pl.pallas_call(layer_kernel, out_shape=jax.ShapeDtypeStruct((OWN, WIDTH),...  48 us
    unnamed x1, local copies, waits for them, and re-layouts  1.38 us

profile of v4, /device:TPU:1, one launch (start us, length us, event | category | flops | bytes accessed | tf_op | source)
XLA Modules:
  0.0 50.0 jit_solution(2310982190443789356)
XLA Ops:
  0.7 48.0 %layer.1 = bf16[64,256]{1,0:T(8,128)(2,1)} custom-call(bf16[64,256]{1,0:T(8,128)(2,1)} %bitcast.5, bf16[64,256]{1,0:T(8,128)(2,1)} %tgt_hbm.1, bf16[256,256]{1,0:T(8,128)(2,1)} %weight_hbm.1, f32[4,64]{1,0:T(4,128)} %source_hbm.1, f32[4,64]{1,0:T(4,128)} %target_hbm.1, f32[1,256]{1,0:T(1,128)} %bitcast.6, s32[1,48]{1,0:T(1,128)} %bitcast.7, ...), custom_call_target="tpu_custom_call" | custom-call | tf_op jit(solution)/shard_map/layer/pallas_call | solution.py:381
  48.7 1.4 %copy.12 = bf16[64,256]{1,0:T(8,128)(2,1)} copy(bf16[64,256]{1,0:T(8,128)(2,1)} %layer.1) | data formatting | bytes 65536

commit v5 on v4

--- a/solution.py
+++ b/solution.py
@@ -63,7 +63,7 @@
     src_ref, tgt_ref, weight_ref, source_ref, target_ref, bias_ref, slots_ref, live_ref, bits_ref,
     feats, src_rows, dst_half, dst, place_rows, places, everyone, spread, tops, maxima, turned,
     weights, slot_sums, products, accum, sent, stats, twin_sent, twin_stats,
-    joint, joint_stats, got, got_stats, half_ref, twin_half,
+    joint, joint_stats, got, got_stats, half_ref, kept_half,
     local, send_ay, recv_ay, send_ax, recv_ax, send_b, recv_b, send_y, recv_y, send_x, recv_x,
     send_p, recv_p, send_j, recv_j, send_k, recv_k, send_one, recv_one,
 ):
@@ -137,7 +137,8 @@
         return send(joint_stats.at[lax.rem(z + d, ZS)], got_stats.at[z], (send_k.at[d], recv_k.at[d]), at_z(d))
 
     def result_pair():
-        return send(half_ref, twin_half, (send_one.at[2], recv_one.at[2]), twin)
+        here = out_ref.at[:, pl.ds(pl.multiple_of(core * BLK, BLK), BLK)]
+        return send(half_ref, here, (send_one.at[2], recv_one.at[2]), twin)
 
     for load in loads[:3]:
         load.wait()
@@ -353,7 +354,9 @@
     result = jnp.where(blended > 0, blended, jnp.exp(jnp.minimum(blended, 0.0)) - 1.0).astype(jnp.bfloat16)
     half_ref[...] = jnp.where(core == 0, result[OWN:], result[:OWN])
     result_pair().start()
-    out_ref[:, pl.ds(pl.multiple_of(core * BLK, BLK), BLK)] = jnp.where(core == 0, result[:OWN], result[OWN:])
+    kept_half[...] = jnp.where(core == 0, result[:OWN], result[OWN:])
+    keep = pltpu.make_async_copy(kept_half, out_ref.at[:, pl.ds(pl.multiple_of(core * BLK, BLK), BLK)], local.at[10])
+    keep.start()
 
     for d in range(1, YS):
         logits_y(d).wait_send()
@@ -370,8 +373,8 @@
         stats_z(d).wait_send()
         sums_z(d).wait_send()
     loop(0, ZS, lambda d: sums_pair(d).wait_send())
+    keep.wait()
     result_pair().wait()
-    out_ref[:, pl.ds(pl.multiple_of((1 - core) * BLK, BLK), BLK)] = twin_half[...]
 
 
 def layer(source, target, weight, score_source, score_target, bias, slots, live, bits):
@@ -380,7 +383,7 @@
     f32, bf16 = jnp.float32, jnp.bfloat16
     return pl.pallas_call(
         layer_kernel,
-        out_shape=jax.ShapeDtypeStruct((OWN, WIDTH), bf16),
+        out_shape=pltpu.VMEM((OWN, WIDTH), bf16),
         in_specs=[pl.BlockSpec(memory_space=pltpu.HBM)] * 9,
         out_specs=pl.BlockSpec(memory_space=pltpu.VMEM),
         scratch_shapes=[
@@ -418,7 +421,7 @@
             vmem((DB, 8, BLK), f32),
             vmem((OWN, BLK), bf16),
             vmem((OWN, BLK), bf16),
-            dma((10,)),
+            dma((11,)),
             dma((YS,)), dma((YS,)),
             dma((XS,)), dma((XS,)),
             dma((ZS,)), dma((ZS,)),

time: 50.2 us -> 48.8 us (0.972)
  local copies, waits for them, and re-layouts: 1.38 us -> 0.62 us
  Pallas kernels: 48 us -> 47.4 us
    unnamed x1, local copies, waits for them, and re-layouts: 1.38 us -> 0.62 us
    pallas_call x1, Pallas kernels: 48 us -> 47.4 us  [layer(): pl.pallas_call(layer_kernel, out_shape=pltpu.VMEM((OWN, WIDTH), bf16), in...]
where the time goes in v5:
time: 48.8 us; the launch traced here: 48.7 us
  Pallas kernels  47.4 us (97%)
  between operations  0.66 us (1%)
  local copies, waits for them, and re-layouts  0.62 us (1%)
    pallas_call x1, Pallas kernels, layer(): pl.pallas_call(layer_kernel, out_shape=pltpu.VMEM((OWN, WIDTH), bf16), in...  47.4 us

profile of v5, /device:TPU:1, one launch (start us, length us, event | category | flops | bytes accessed | tf_op | source)
XLA Modules:
  0.0 48.7 jit_solution(5634300282656577701)
XLA Ops:
  0.7 47.4 %layer.1 = bf16[64,256]{1,0:T(8,128)(2,1)S(1)} custom-call(bf16[64,256]{1,0:T(8,128)(2,1)} %bitcast.5, bf16[64,256]{1,0:T(8,128)(2,1)} %tgt_hbm.1, bf16[256,256]{1,0:T(8,128)(2,1)} %weight_hbm.1, f32[4,64]{1,0:T(4,128)} %source_hbm.1, f32[4,64]{1,0:T(4,128)} %target_hbm.1, f32[1,256]{1,0:T(1,128)} %bitcast.6, s32[1,48]{1,0:T(1,128)} %bitcast.7, ...), custom_call_target="tpu_custom_call" | custom-call | tf_op jit(solution)/shard_map/layer/pallas_call | solution.py:384
  48.1 0.6 %copy.11 = bf16[64,256]{1,0:T(8,128)(2,1)} copy(bf16[64,256]{1,0:T(8,128)(2,1)S(1)} %layer.1) | data formatting | bytes 65536

commit v6 on v5

--- a/solution.py
+++ b/solution.py
@@ -334,6 +334,20 @@
             got_stats[z] = tile
             got[z] = mixed
 
+    for d in range(1, YS):
+        logits_y(d).wait_send()
+        feats_y(d).wait_send()
+    for e in range(1, XS):
+        logits_x(e).wait_send()
+    for d in range(YS):
+        for e in range(1, XS):
+            feats_x(d, e).wait_send()
+    target_pair().wait_send()
+    stats_pair().wait_send()
+    for d in range(1, ZS):
+        target_z(d).wait_send()
+    loop(0, ZS, lambda d: sums_pair(d).wait_send())
+
     for d in range(1, ZS):
         stats_z(d).wait_recv()
     every = got_stats[...]
@@ -358,21 +372,9 @@
     keep = pltpu.make_async_copy(kept_half, out_ref.at[:, pl.ds(pl.multiple_of(core * BLK, BLK), BLK)], local.at[10])
     keep.start()
 
-    for d in range(1, YS):
-        logits_y(d).wait_send()
-        feats_y(d).wait_send()
-    for e in range(1, XS):
-        logits_x(e).wait_send()
-    for d in range(YS):
-        for e in range(1, XS):
-            feats_x(d, e).wait_send()
-    target_pair().wait_send()
-    stats_pair().wait_send()
-    for d in range(1, ZS):
-        target_z(d).wait_send()
+    for d in range(1, ZS):
         stats_z(d).wait_send()
         sums_z(d).wait_send()
-    loop(0, ZS, lambda d: sums_pair(d).wait_send())
     keep.wait()
     result_pair().wait()
 

time: 48.8 us -> 48.8 us (level)
  no operation moved by 1% of the time
where the time goes in v6:
time: 48.8 us; the launch traced here: 48.7 us
  Pallas kernels  47.4 us (97%)
  between operations  0.66 us (1%)
  local copies, waits for them, and re-layouts  0.62 us (1%)
    pallas_call x1, Pallas kernels, layer(): pl.pallas_call(layer_kernel, out_shape=pltpu.VMEM((OWN, WIDTH), bf16), in...  47.4 us

profile of v6, /device:TPU:1, one launch (start us, length us, event | category | flops | bytes accessed | tf_op | source)
XLA Modules:
  0.0 48.7 jit_solution(14277340451132484082)
XLA Ops:
  0.7 47.4 %layer.1 = bf16[64,256]{1,0:T(8,128)(2,1)S(1)} custom-call(bf16[64,256]{1,0:T(8,128)(2,1)} %bitcast.5, bf16[64,256]{1,0:T(8,128)(2,1)} %tgt_hbm.1, bf16[256,256]{1,0:T(8,128)(2,1)} %weight_hbm.1, f32[4,64]{1,0:T(4,128)} %source_hbm.1, f32[4,64]{1,0:T(4,128)} %target_hbm.1, f32[1,256]{1,0:T(1,128)} %bitcast.6, s32[1,48]{1,0:T(1,128)} %bitcast.7, ...), custom_call_target="tpu_custom_call" | custom-call | tf_op jit(solution)/shard_map/layer/pallas_call | solution.py:386
  48.1 0.6 %copy.11 = bf16[64,256]{1,0:T(8,128)(2,1)} copy(bf16[64,256]{1,0:T(8,128)(2,1)S(1)} %layer.1) | data formatting | bytes 65536
